TPU v7x, 32 devices: a whole 2x2x4 slice. The times are simulated.
32 devices in a mesh: blk: 2 (over x), tp: 4 (over y, core), enc: 4 (over z).
Axes of the slice: x: 2, y: 2, z: 4, core: 2. Of those that a mesh axis runs over, the one named last changes fastest.
Arguments:
- self_query_columns: bfloat16 [1024, 4096], P('blk', ('tp', 'enc')), may hold values from -12 to 12
- text_key_value: bfloat16 [1024, 2, 512], P('blk', None, 'tp'), may hold values from -9 to 9
- cross_query_columns: bfloat16 [1024, 4096], P('blk', ('tp', 'enc')), may hold values from -12 to 12
- image_kv: bfloat16 [2, 2, 6404, 512], P('blk', None, 'enc', 'tp'), may hold values from -9 to 9
- block_images: int32 [8, 2], P('blk'), may hold values from 0 to 1, as said below
- image_owner: int32 [2], replicated, may hold values from 0 to 1, each once
Outputs:
- self_out: bfloat16 [1024, 4096], P('blk', ('tp', 'enc'))
- cross_out: bfloat16 [1024, 4096], P('blk', ('tp', 'enc'))
Inputs may be any that keep to these rules, and one draw needn't show every extreme that they name: `block_images`: each block of 128 text tokens sees one or two images: the image most recently placed before it and, in some blocks, the image placed before that one. Image ids rise along the text, every image is seen by some block, and some block sees two. A permutation: image i's keys and values are slot image_owner[i] of image_kv.
All inputs are finite; a program needn't handle non-finite values.
Results may differ from a plain program's by a relative error of at most 0.007.
Values may be sent and summed in bfloat16 or wider, within the bound.
No kernel may reach another device: no remote copies, remote signals or barrier semaphores. Data moves between devices by JAX's collectives and lax.ppermute only.
A program may use at most 64 MiB of HBM per device.

v0:
```python
import functools
import math

import jax
import jax.numpy as jnp
from jax import lax
from jax.experimental import pallas as pl
from jax.experimental.pallas import tpu as pltpu
from jax.sharding import PartitionSpec as P

HEAD_SIZE = 128
MASK_BLOCK_TOKENS = 128
LANES = 128
LOWEST = -1e30
LOG2_SCALE = math.log2(math.e) / math.sqrt(HEAD_SIZE)
VMEM_LIMIT = 48 * 1024 * 1024

VMEM = pl.BlockSpec(memory_space=pltpu.VMEM)
SMEM = pl.BlockSpec(memory_space=pltpu.SMEM)


def padded(count):
    return -(-count // LANES) * LANES


def nt_dot(a, b):
    return lax.dot_general(a, b, (((1,), (1,)), ((), ())), preferred_element_type=jnp.float32)


def at_block(block):
    return pl.ds(pl.multiple_of(block * MASK_BLOCK_TOKENS, MASK_BLOCK_TOKENS), MASK_BLOCK_TOKENS)


def stacked_heads(rows):
    heads = rows.shape[1] // HEAD_SIZE
    return jnp.concatenate([rows[:, h * HEAD_SIZE : (h + 1) * HEAD_SIZE] for h in range(heads)], axis=0)


def lane_tiles(wide):
    return [wide[:, at : at + LANES] for at in range(0, wide.shape[1], LANES)]


def empty_state(rows):
    return (
        jnp.full((rows, 1), LOWEST, jnp.float32),
        jnp.zeros((rows, LANES), jnp.float32),
        jnp.zeros((rows, HEAD_SIZE), jnp.float32),
    )


def fold(state, scores, value):
    high, total, mixed = state
    new_high = jnp.maximum(high, jnp.max(functools.reduce(jnp.maximum, lane_tiles(scores)), axis=1, keepdims=True))
    weights = jnp.exp2(scores * LOG2_SCALE - new_high * LOG2_SCALE)
    fading = jnp.exp2((high - new_high) * LOG2_SCALE)
    total = total * fading + functools.reduce(jnp.add, lane_tiles(weights))
    mixed = mixed * fading + jnp.dot(weights.astype(jnp.bfloat16), value, preferred_element_type=jnp.float32)
    return (new_high, total, mixed)


def prepare_kernel(kv_ref, out_ref):
    count = kv_ref.shape[1]
    whole = count // LANES * LANES
    rest = count - whole
    for at in range(0, whole, LANES):
        out_ref[0, at : at + LANES, :] = kv_ref[0, at : at + LANES, :].T
    out_ref[1, 0:whole, :] = kv_ref[1, 0:whole, :]
    if rest:
        empty = jnp.zeros((LANES - rest, HEAD_SIZE), jnp.float32)
        tail_key = jnp.concatenate([kv_ref[0, whole:count, :].astype(jnp.float32), empty], axis=0)
        tail_value = jnp.concatenate([kv_ref[1, whole:count, :].astype(jnp.float32), empty], axis=0)
        out_ref[0, whole : whole + LANES, :] = tail_key.T.astype(jnp.bfloat16)
        out_ref[1, whole : whole + LANES, :] = tail_value.astype(jnp.bfloat16)


def prepare(kv):
    return pl.pallas_call(
        prepare_kernel,
        out_shape=jax.ShapeDtypeStruct((2, padded(kv.shape[1]), HEAD_SIZE), jnp.bfloat16),
        in_specs=[VMEM],
        out_specs=VMEM,
        compiler_params=pltpu.CompilerParams(vmem_limit_bytes=VMEM_LIMIT),
        cost_estimate=pl.CostEstimate(flops=0, bytes_accessed=2 * kv.size * 2, transcendentals=0),
        name="prepare",
    )(kv)


def chunk_starts(width):
    half = width // LANES // 2 * LANES
    return [(0, half), (half, width)] if half else [(0, width)]


def lse_rows(block_count):
    return -(-3 * block_count // 16) * 16


def cross_kernel(key_count, pieces, offset, last, position_ref, images_ref, owner_ref, q_ref, *refs):
    images, refs = refs[:pieces], refs[pieces:]
    if offset:
        before, refs = refs[:3], refs[3:]
    if last:
        out_ref, lse_ref = refs[0], refs[1]
        state_refs = refs[2:]
        lse_ref[...] = jnp.zeros_like(lse_ref)
    else:
        state_refs = refs
    slots = images_ref.shape[1]
    block_count = q_ref.shape[0] // MASK_BLOCK_TOKENS
    heads = q_ref.shape[1] // HEAD_SIZE
    rows = heads * MASK_BLOCK_TOKENS

    def per_block(block, carry):
        at = pl.ds(pl.multiple_of(block * rows, rows), rows)
        here = at if not last else slice(None)
        if offset:
            for ref, old in zip(state_refs, before):
                ref[here, :] = old[at, :]
        else:
            for ref, value in zip(state_refs, empty_state(rows)):
                ref[here, :] = jnp.broadcast_to(value, (rows, LANES))
        for piece in range(pieces):
            slot = lax.rem(position_ref[0] + (slots - offset - piece), slots)
            seen = jnp.int32(0)
            for image in range(slots):
                seen = seen + jnp.where(owner_ref[image] == slot, images_ref[block, image], 0)

            @pl.when(seen > 0)
            def _(piece=piece):
                image = images[piece]
                queries = stacked_heads(q_ref[at_block(block), :])
                state = (state_refs[0][here, 0:1], state_refs[1][here, :], state_refs[2][here, :])
                for start, stop in chunk_starts(image.shape[1]):
                    keys = jnp.concatenate(
                        [image[0, c : c + LANES, :] for c in range(start, stop, LANES)], axis=1
                    )
                    scores = jnp.dot(queries, keys, preferred_element_type=jnp.float32)
                    if stop > key_count:
                        key_id = start + lax.broadcasted_iota(jnp.int32, scores.shape, 1)
                        scores = jnp.where(key_id < key_count, scores, LOWEST)
                    state = fold(state, scores, image[1, start:stop, :])
                for ref, value in zip(state_refs, state):
                    ref[here, :] = jnp.broadcast_to(value, (rows, LANES))

        if last:
            total = jnp.sum(state_refs[1][...], axis=1, keepdims=True)
            mixed = state_refs[2][...] / total
            lse = state_refs[0][...] * LOG2_SCALE + jnp.log2(total)
            for head in range(heads):
                own = slice(head * MASK_BLOCK_TOKENS, (head + 1) * MASK_BLOCK_TOKENS)
                out_ref[at_block(block), head * HEAD_SIZE : (head + 1) * HEAD_SIZE] = mixed[own].astype(jnp.bfloat16)
                row = lax.broadcasted_iota(jnp.int32, (lse_ref.shape[0], MASK_BLOCK_TOKENS), 0)
                lse_ref[:, own] = jnp.where(row == block, lse[own].T[0:1, :], lse_ref[:, own])
        return carry

    lax.fori_loop(0, block_count, per_block, 0)
    if last:
        lse = lse_ref[...]
        first = lse.astype(jnp.bfloat16).astype(jnp.float32)
        second = (lse - first).astype(jnp.bfloat16).astype(jnp.float32)
        third = lse - first - second
        parts = [part[0:block_count, :] for part in (first, second, third)]
        spare = lse_rows(block_count) - 3 * block_count
        if spare:
            parts.append(jnp.zeros((spare, rows), jnp.float32))
        out_ref[q_ref.shape[0] :, :] = jnp.concatenate(parts, axis=0).astype(jnp.bfloat16)


def cross_part(tables, queries, images, key_count, offset, last, before=()):
    tokens, columns = queries.shape
    block_count = tokens // MASK_BLOCK_TOKENS
    rows = columns // HEAD_SIZE * MASK_BLOCK_TOKENS
    if last:
        out_shape = jax.ShapeDtypeStruct((tokens + lse_rows(block_count), columns), jnp.bfloat16)
        scratch = [pltpu.VMEM((-(-block_count // 8) * 8, rows), jnp.float32)]
        scratch += [pltpu.VMEM((rows, LANES), jnp.float32)] * 3
    else:
        out_shape = (jax.ShapeDtypeStruct((block_count * rows, LANES), jnp.float32),) * 3
        scratch = []
    flops = 4 * block_count * rows * key_count * HEAD_SIZE * len(images)
    return pl.pallas_call(
        functools.partial(cross_kernel, key_count, len(images), offset, last),
        out_shape=out_shape,
        in_specs=[SMEM, SMEM, SMEM] + [VMEM] * (1 + len(images) + len(before)),
        out_specs=VMEM if last else (VMEM,) * 3,
        scratch_shapes=scratch,
        compiler_params=pltpu.CompilerParams(vmem_limit_bytes=VMEM_LIMIT),
        cost_estimate=pl.CostEstimate(flops=2 * flops, bytes_accessed=4 * 1024 * 1024, transcendentals=0),
        name="cross_last" if last else "cross_first",
    )(*tables, queries, *images, *before)


def combine_kernel(parts, *refs):
    part_refs, out_ref = refs[:parts], refs[parts]
    tokens, columns = out_ref.shape
    block_count = tokens // MASK_BLOCK_TOKENS
    heads = columns // HEAD_SIZE
    lse = []
    for ref in part_refs:
        tail = ref[tokens:, :].astype(jnp.float32)
        lse.append(
            tail[0:block_count] + tail[block_count : 2 * block_count] + tail[2 * block_count : 3 * block_count]
        )
    highest = functools.reduce(jnp.maximum, lse)
    weights = [jnp.exp2(one - highest) for one in lse]
    total = functools.reduce(jnp.add, weights)
    by_row = [
        (one / total)[:, head * MASK_BLOCK_TOKENS : (head + 1) * MASK_BLOCK_TOKENS]
        for one in weights
        for head in range(heads)
    ]
    used = len(by_row) * block_count
    by_row.append(jnp.zeros((padded(used) - used, MASK_BLOCK_TOKENS), jnp.float32))
    columns_of = jnp.concatenate(by_row, axis=0).T
    for block in range(block_count):
        at = slice(block * MASK_BLOCK_TOKENS, (block + 1) * MASK_BLOCK_TOKENS)
        for head in range(heads):
            dims = slice(head * HEAD_SIZE, (head + 1) * HEAD_SIZE)
            mixed = 0.0
            for index, ref in enumerate(part_refs):
                column = (index * heads + head) * block_count + block
                mixed = mixed + columns_of[:, column : column + 1] * ref[at, dims].astype(jnp.float32)
            out_ref[at, dims] = mixed.astype(jnp.bfloat16)


def combined(parts, shape):
    return pl.pallas_call(
        functools.partial(combine_kernel, len(parts)),
        out_shape=jax.ShapeDtypeStruct(shape, jnp.bfloat16),
        in_specs=[VMEM] * len(parts),
        out_specs=VMEM,
        compiler_params=pltpu.CompilerParams(vmem_limit_bytes=VMEM_LIMIT),
        cost_estimate=pl.CostEstimate(flops=0, bytes_accessed=2 * 1024 * 1024, transcendentals=0),
        name="combine",
    )(*parts)


def self_kernel(pieces, position_ref, q_ref, *refs):
    texts = refs[:pieces]
    out_ref, high_ref, total_ref, mixed_ref = refs[pieces:]
    tokens, columns = q_ref.shape
    heads = columns // HEAD_SIZE
    rows = heads * MASK_BLOCK_TOKENS
    state_refs = (high_ref, total_ref, mixed_ref)
    for block in range(tokens // MASK_BLOCK_TOKENS):
        start = block * MASK_BLOCK_TOKENS
        stop = start + MASK_BLOCK_TOKENS
        queries = stacked_heads(q_ref[start:stop, :])
        scores = nt_dot(queries, texts[0][0:stop, 0:HEAD_SIZE])
        key_id = lax.broadcasted_iota(jnp.int32, scores.shape, 1)
        query_id = start + lax.broadcasted_iota(jnp.int32, scores.shape, 0) % MASK_BLOCK_TOKENS
        scores = jnp.where(key_id <= query_id, scores, LOWEST)
        state = fold(empty_state(rows), scores, texts[0][0:stop, HEAD_SIZE:])
        for ref, value in zip(state_refs, state):
            ref[...] = jnp.broadcast_to(value, (rows, LANES))
        for piece in range(1, pieces):

            @pl.when(position_ref[0] >= piece)
            def _(piece=piece):
                scores = nt_dot(queries, texts[piece][:, 0:HEAD_SIZE])
                state = fold((high_ref[:, 0:1], total_ref[...], mixed_ref[...]), scores, texts[piece][:, HEAD_SIZE:])
                for ref, value in zip(state_refs, state):
                    ref[...] = jnp.broadcast_to(value, (rows, LANES))

        mixed = mixed_ref[...] / jnp.sum(total_ref[...], axis=1, keepdims=True)
        for head in range(heads):
            out_ref[start:stop, head * HEAD_SIZE : (head + 1) * HEAD_SIZE] = mixed[
                head * MASK_BLOCK_TOKENS : (head + 1) * MASK_BLOCK_TOKENS
            ].astype(jnp.bfloat16)


def self_attention(position, queries, texts):
    tokens, columns = queries.shape
    pieces = len(texts)
    rows = columns // HEAD_SIZE * MASK_BLOCK_TOKENS
    return pl.pallas_call(
        functools.partial(self_kernel, pieces),
        out_shape=jax.ShapeDtypeStruct((tokens, columns), jnp.bfloat16),
        in_specs=[SMEM] + [VMEM] * (1 + pieces),
        out_specs=VMEM,
        scratch_shapes=[pltpu.VMEM((rows, LANES), jnp.float32)] * 3,
        compiler_params=pltpu.CompilerParams(vmem_limit_bytes=VMEM_LIMIT),
        cost_estimate=pl.CostEstimate(flops=8 * tokens * columns * tokens, bytes_accessed=1024 * 1024, transcendentals=0),
        name="self_attention",
    )(position, queries, *texts)


def shifted(value, axis, steps):
    count = lax.axis_size(axis)
    return lax.ppermute(value, axis, [(source, (source + steps) % count) for source in range(count)])


def per_device(self_queries, text_kv, cross_queries, image_kv, block_images, image_owner):
    rows = self_queries.shape[0]
    key_count = image_kv.shape[2]
    cycle = lax.axis_size("blk")
    ring = lax.axis_size("enc")
    position = lax.axis_index("blk").astype(jnp.int32)[None]

    tables = (position, block_images, image_owner)

    images = [prepare(image_kv[0])]
    for _ in range(1, cycle):
        images.append(shifted(images[-1], "blk", 1))
    order = sorted(range(1, ring), key=lambda step: (abs(2 * step - ring), step))
    queries = {step: shifted(cross_queries, "enc", ring - step) for step in order}
    queries[0] = cross_queries

    alone = cycle == 1
    states = {}
    for step in [0] + order:
        states[step] = () if alone else cross_part(tables, queries[step], images[:1], key_count, 0, False)

    def finished(step):
        offset = 0 if alone else 1
        return cross_part(tables, queries[step], images[offset:], key_count, offset, True, states[step])

    received = [shifted(finished(step), "enc", step) for step in order]

    text = text_kv.reshape(rows, 2 * HEAD_SIZE)
    after, _ = lax.optimization_barrier((text, images[-1]))
    texts = [text]
    for step in range(1, cycle):
        after = lax.ppermute(after, "blk", [(source, source + 1) for source in range(cycle - 1)])
        texts.append(after)

    own = finished(0)
    self_out = self_attention(position, self_queries, texts)
    cross_out = combined([own] + received, cross_queries.shape)
    return (self_out, cross_out)


def solution(mesh):
    placed = (
        P("blk", ("tp", "enc")),
        P("blk", None, "tp"),
        P("blk", ("tp", "enc")),
        P("blk", None, "enc", "tp"),
        P("blk", None),
        P(),
    )
    return jax.shard_map(
        per_device,
        mesh=mesh,
        in_specs=placed,
        out_specs=(P("blk", ("tp", "enc")), P("blk", ("tp", "enc"))),
        check_vma=False,
    )
```

profile of v0, /device:TPU:6, one launch (start us, length us, event | category | flops | bytes accessed | tf_op | source)
XLA Modules:
  0.0 75.3 jit_solution(16068696068975186870)
XLA Ops:
  0.6 1.3 %copy.20 = bf16[1,2,1601,128]{3,2,1,0:T(8,128)(2,1)S(1)} copy(bf16[1,2,1601,128]{3,1,2,0:T(2,128)(2,1)} %param.9) | data formatting | bytes 1639424 | tf_op args[3]
  1.9 0.0 copy-start
  1.9 0.0 copy-start.3
  1.9 0.2 prepare.1.refs_0_
  2.1 0.6 collective-permute-start
  2.7 0.1 copy-done
  2.8 1.6 %collective-permute-start.6 = (bf16[512,256]{1,0:T(8,128)(2,1)S(1)}, bf16[512,256]{1,0:T(8,128)(2,1)S(1)}, u32[]{:S(2)}, u32[]{:S(2)}) collective-permute-start(bf16[512,256]{1,0:T(8,128)(2,1)S(1)} %copy-done), channel_id=1, source_target_pairs={{0,1},{1,2},{2,3},{3,0},{4,5},{5,6},{6,7},{7,4},{8,9},{9,10},{10,1... | collective-permute-start | bytes 786440 | tf_op jit(solution)/shard_map/ppermute | solution.py:289
  4.4 2.2 %collective-permute-start.4 = (bf16[512,256]{1,0:T(8,128)(2,1)S(1)}, bf16[512,256]{1,0:T(8,128)(2,1)S(1)}, u32[]{:S(2)}, u32[]{:S(2)}) collective-permute-start(bf16[512,256]{1,0:T(8,128)(2,1)S(1)} %copy-done), channel_id=1, source_target_pairs={{0,3},{1,0},{2,1},{3,2},{4,7},{5,4},{6,5},{7,6},{8,11},{9,8},{10,9... | collective-permute-start | bytes 786440 | tf_op jit(solution)/shard_map/ppermute | solution.py:289
  6.7 0.8 %collective-permute-start.2 = (bf16[512,256]{1,0:T(8,128)(2,1)S(1)}, bf16[512,256]{1,0:T(8,128)(2,1)S(1)}, u32[]{:S(2)}, u32[]{:S(2)}) collective-permute-start(bf16[512,256]{1,0:T(8,128)(2,1)S(1)} %copy-done), channel_id=1, source_target_pairs={{0,2},{1,3},{2,0},{3,1},{4,6},{5,7},{6,4},{7,5},{8,10},{9,11},{10,... | collective-permute-start | bytes 786440 | tf_op jit(solution)/shard_map/ppermute | solution.py:289
  7.5 0.0 copy-start.4
  7.5 0.7 copy-done.4
  8.1 0.1 copy.10.images_ref
  8.2 0.0 copy-done.3
  8.3 0.0 copy-start.2
  8.3 5.6 %collective-permute-done.6.q_ref = bf16[512,256]{1,0:T(8,128)(2,1)S(1)} collective-permute-done((bf16[512,256]{1,0:T(8,128)(2,1)S(1)}, bf16[512,256]{1,0:T(8,128)(2,1)S(1)}, u32[]{:S(2)}, u32[]{:S(2)}) %collective-permute-start.6) | collective-permute-done | bytes 262176 | tf_op jit(solution)/shard_map/ppermute | solution.py:289
  13.9 0.0 copy-done.2
  13.9 3.3 %cross_first.7 = (f32[1024,128]{1,0:T(8,128)S(1)}, f32[1024,128]{1,0:T(8,128)S(1)}, f32[1024,128]{1,0:T(8,128)S(1)}) custom-call(s32[1]{0:T(128)} %bitcast.position_ref, s32[4,2]{1,0:T(4,128)S(1)} %copy.10.images_ref, s32[2]{0:T(128)S(1)} %copy-done.2, bf16[512,256]{1,0:T(8,128)(2,1)S(1)} %collective-permute-done.6.q_ref, ...), custom_call_target="tpu_custom_call" | custom-call | flops 1678770176 | bytes 4194304 | tf_op jit(solution)/shard_map/cross_first/pallas_call | solution.py:180
  17.2 0.6 collective-permute-done.4.q_ref
  17.8 3.3 %cross_first.6 = (f32[1024,128]{1,0:T(8,128)S(1)}, f32[1024,128]{1,0:T(8,128)S(1)}, f32[1024,128]{1,0:T(8,128)S(1)}) custom-call(s32[1]{0:T(128)} %bitcast.position_ref, s32[4,2]{1,0:T(4,128)S(1)} %copy.10.images_ref, s32[2]{0:T(128)S(1)} %copy-done.2, bf16[512,256]{1,0:T(8,128)(2,1)S(1)} %collective-permute-done.4.q_ref, ...), custom_call_target="tpu_custom_call" | custom-call | flops 1678770176 | bytes 4194304 | tf_op jit(solution)/shard_map/cross_first/pallas_call | solution.py:180
  21.1 8.5 %collective-permute-done.2.q_ref = bf16[512,256]{1,0:T(8,128)(2,1)S(1)} collective-permute-done((bf16[512,256]{1,0:T(8,128)(2,1)S(1)}, bf16[512,256]{1,0:T(8,128)(2,1)S(1)}, u32[]{:S(2)}, u32[]{:S(2)}) %collective-permute-start.2) | collective-permute-done | bytes 262176 | tf_op jit(solution)/shard_map/ppermute | solution.py:289
  29.6 3.3 %cross_first.5 = (f32[1024,128]{1,0:T(8,128)S(1)}, f32[1024,128]{1,0:T(8,128)S(1)}, f32[1024,128]{1,0:T(8,128)S(1)}) custom-call(s32[1]{0:T(128)} %bitcast.position_ref, s32[4,2]{1,0:T(4,128)S(1)} %copy.10.images_ref, s32[2]{0:T(128)S(1)} %copy-done.2, bf16[512,256]{1,0:T(8,128)(2,1)S(1)} %collective-permute-done.2.q_ref, ...), custom_call_target="tpu_custom_call" | custom-call | flops 1678770176 | bytes 4194304 | tf_op jit(solution)/shard_map/cross_first/pallas_call | solution.py:180
  32.9 0.0 collective-permute-done.refs_0_
  32.9 6.5 %cross_last.7 = bf16[528,256]{1,0:T(8,128)(2,1)S(1)} custom-call(s32[1]{0:T(128)} %bitcast.position_ref, s32[4,2]{1,0:T(4,128)S(1)} %copy.10.images_ref, s32[2]{0:T(128)S(1)} %copy-done.2, bf16[512,256]{1,0:T(8,128)(2,1)S(1)} %collective-permute-done.6.q_ref, bf16[2,1664,128]{2,1,0:T(8,128)(2,1)S(1)} %collective-permute-done.refs_0_, ...), custom_call_target="tpu_custom_call" | custom-call | flops 1678770176 | bytes 4194304 | tf_op jit(solution)/shard_map/cross_last/pallas_call | solution.py:180
  39.5 1.7 %collective-permute-start.7 = (bf16[528,256]{1,0:T(8,128)(2,1)S(1)}, bf16[528,256]{1,0:T(8,128)(2,1)S(1)}, u32[]{:S(2)}, u32[]{:S(2)}) collective-permute-start(bf16[528,256]{1,0:T(8,128)(2,1)S(1)} %cross_last.7), channel_id=1, source_target_pairs={{0,3},{1,0},{2,1},{3,2},{4,7},{5,4},{6,5},{7,6},{8,11},{9,8},{10,9... | collective-permute-start | bytes 811016 | tf_op jit(solution)/shard_map/ppermute | solution.py:289
  41.1 6.5 %cross_last.6 = bf16[528,256]{1,0:T(8,128)(2,1)S(1)} custom-call(s32[1]{0:T(128)} %bitcast.position_ref, s32[4,2]{1,0:T(4,128)S(1)} %copy.10.images_ref, s32[2]{0:T(128)S(1)} %copy-done.2, bf16[512,256]{1,0:T(8,128)(2,1)S(1)} %collective-permute-done.4.q_ref, bf16[2,1664,128]{2,1,0:T(8,128)(2,1)S(1)} %collective-permute-done.refs_0_, ...), custom_call_target="tpu_custom_call" | custom-call | flops 1678770176 | bytes 4194304 | tf_op jit(solution)/shard_map/cross_last/pallas_call | solution.py:180
  47.6 0.5 collective-permute-start.5
  48.1 6.5 %cross_last.5 = bf16[528,256]{1,0:T(8,128)(2,1)S(1)} custom-call(s32[1]{0:T(128)} %bitcast.position_ref, s32[4,2]{1,0:T(4,128)S(1)} %copy.10.images_ref, s32[2]{0:T(128)S(1)} %copy-done.2, bf16[512,256]{1,0:T(8,128)(2,1)S(1)} %collective-permute-done.2.q_ref, bf16[2,1664,128]{2,1,0:T(8,128)(2,1)S(1)} %collective-permute-done.refs_0_, ...), custom_call_target="tpu_custom_call" | custom-call | flops 1678770176 | bytes 4194304 | tf_op jit(solution)/shard_map/cross_last/pallas_call | solution.py:180
  54.6 3.0 %collective-permute-start.3 = (bf16[528,256]{1,0:T(8,128)(2,1)S(1)}, bf16[528,256]{1,0:T(8,128)(2,1)S(1)}, u32[]{:S(2)}, u32[]{:S(2)}) collective-permute-start(bf16[528,256]{1,0:T(8,128)(2,1)S(1)} %cross_last.5), channel_id=1, source_target_pairs={{0,2},{1,3},{2,0},{3,1},{4,6},{5,7},{6,4},{7,5},{8,10},{9,11},{10,... | collective-permute-start | bytes 811016 | tf_op jit(solution)/shard_map/ppermute | solution.py:289
  57.6 1.3 %collective-permute-start.1 = (bf16[512,256]{1,0:T(8,128)(2,1)S(1)}, bf16[512,256]{1,0:T(8,128)(2,1)S(1)}, u32[]{:S(2)}, u32[]{:S(2)}) collective-permute-start(bf16[512,256]{1,0:T(8,128)(2,1)S(1)} %bitcast.9), channel_id=1, source_target_pairs={{0,16},{1,17},{2,18},{3,19},{4,20},{5,21},{6,22},{7,23},{8,24},{9,... | collective-permute-start | bytes 786440 | tf_op jit(solution)/shard_map/ppermute | solution.py:323
  58.9 3.3 %cross_first.4 = (f32[1024,128]{1,0:T(8,128)S(1)}, f32[1024,128]{1,0:T(8,128)S(1)}, f32[1024,128]{1,0:T(8,128)S(1)}) custom-call(s32[1]{0:T(128)} %bitcast.position_ref, s32[4,2]{1,0:T(4,128)S(1)} %copy.10.images_ref, s32[2]{0:T(128)S(1)} %copy-done.2, bf16[512,256]{1,0:T(8,128)(2,1)S(1)} %copy-done, bf16[2,1664,128]{2,1,0:T(8,128)(2,1)S(1)} %prepare.1.refs_0_), custom_call_target="tpu_custom_call" | custom-call | flops 1678770176 | bytes 4194304 | tf_op jit(solution)/shard_map/cross_first/pallas_call | solution.py:180
  62.3 0.0 copy-start.1
  62.3 6.5 %cross_last.4.refs_0_ = bf16[528,256]{1,0:T(8,128)(2,1)S(1)} custom-call(s32[1]{0:T(128)} %bitcast.position_ref, s32[4,2]{1,0:T(4,128)S(1)} %copy.10.images_ref, s32[2]{0:T(128)S(1)} %copy-done.2, bf16[512,256]{1,0:T(8,128)(2,1)S(1)} %copy-done, bf16[2,1664,128]{2,1,0:T(8,128)(2,1)S(1)} %collective-permute-done.refs_0_, ...), custom_call_target="tpu_custom_call" | custom-call | flops 1678770176 | bytes 4194304 | tf_op jit(solution)/shard_map/cross_last/pallas_call | solution.py:180
  68.8 0.0 collective-permute-done.1.refs_1_
  68.8 0.0 copy-done.1
  68.8 5.0 %self_attention.1 = bf16[512,256]{1,0:T(8,128)(2,1)} custom-call(s32[1]{0:T(128)} %bitcast.position_ref, bf16[512,256]{1,0:T(8,128)(2,1)S(1)} %copy-done.1, bf16[512,256]{1,0:T(8,128)(2,1)S(1)} %bitcast.10, bf16[512,256]{1,0:T(8,128)(2,1)S(1)} %collective-permute-done.1.refs_1_), custom_call_target="tpu_custom_call" | custom-call | flops 536870912 | bytes 1048576 | tf_op jit(solution)/shard_map/self_attention/pallas_call | solution.py:275
  73.8 0.0 collective-permute-done.7.refs_3_
  73.8 0.0 collective-permute-done.5.refs_2_
  73.8 0.0 collective-permute-done.3.refs_1_
  73.8 1.5 %combine.1 = bf16[512,256]{1,0:T(8,128)(2,1)} custom-call(bf16[528,256]{1,0:T(8,128)(2,1)S(1)} %cross_last.4.refs_0_, bf16[528,256]{1,0:T(8,128)(2,1)S(1)} %collective-permute-done.3.refs_1_, bf16[528,256]{1,0:T(8,128)(2,1)S(1)} %collective-permute-done.5.refs_2_, bf16[528,256]{1,0:T(8,128)(2,1)S(1)} %collective-permute-done.7.refs_3_), custom_call_target="tpu_custom_call" | custom-call | bytes 2097152 | tf_op jit(solution)/shard_map/combine/pallas_call | solution.py:226
  (1 shorter events, 0.0 us)
Async XLA Ops:
  1.9 1.0 %copy-start = (bf16[512,256]{1,0:T(8,128)(2,1)S(1)}, bf16[512,256]{1,0:T(8,128)(2,1)}, u32[]{:S(2)}) copy-start(bf16[512,256]{1,0:T(8,128)(2,1)} %q_ref.5) | copy-start | bytes 786436
  1.9 6.3 %copy-start.3 = (bf16[512,2,128]{2,1,0:T(2,128)(2,1)S(1)}, bf16[512,2,128]{2,1,0:T(2,128)(2,1)}, u32[]{:S(2)}) copy-start(bf16[512,2,128]{2,1,0:T(2,128)(2,1)} %param.7) | copy-start | bytes 786436
  2.1 30.8 %collective-permute-start = (bf16[2,1664,128]{2,1,0:T(8,128)(2,1)S(1)}, bf16[2,1664,128]{2,1,0:T(8,128)(2,1)S(1)}, u32[]{:S(2)}, u32[]{:S(2)}) collective-permute-start(bf16[2,1664,128]{2,1,0:T(8,128)(2,1)S(1)} %prepare.1.refs_0_), channel_id=1, source_target_pairs={{0,16},{16,0},{1,17},{17,1},{2,18},{18,2},{3,19},{19,3},{4,20},{20... | collective-permute-start | bytes 2555912 | tf_op jit(solution)/shard_map/ppermute | solution.py:289
  2.8 11.0 %collective-permute-start.6 = (bf16[512,256]{1,0:T(8,128)(2,1)S(1)}, bf16[512,256]{1,0:T(8,128)(2,1)S(1)}, u32[]{:S(2)}, u32[]{:S(2)}) collective-permute-start(bf16[512,256]{1,0:T(8,128)(2,1)S(1)} %copy-done), channel_id=1, source_target_pairs={{0,1},{1,2},{2,3},{3,0},{4,5},{5,6},{6,7},{7,4},{8,9},{9,10},{10,1... | collective-permute-start | bytes 786440 | tf_op jit(solution)/shard_map/ppermute | solution.py:289
  4.4 13.4 %collective-permute-start.4 = (bf16[512,256]{1,0:T(8,128)(2,1)S(1)}, bf16[512,256]{1,0:T(8,128)(2,1)S(1)}, u32[]{:S(2)}, u32[]{:S(2)}) collective-permute-start(bf16[512,256]{1,0:T(8,128)(2,1)S(1)} %copy-done), channel_id=1, source_target_pairs={{0,3},{1,0},{2,1},{3,2},{4,7},{5,4},{6,5},{7,6},{8,11},{9,8},{10,9... | collective-permute-start | bytes 786440 | tf_op jit(solution)/shard_map/ppermute | solution.py:289
  6.7 22.9 %collective-permute-start.2 = (bf16[512,256]{1,0:T(8,128)(2,1)S(1)}, bf16[512,256]{1,0:T(8,128)(2,1)S(1)}, u32[]{:S(2)}, u32[]{:S(2)}) collective-permute-start(bf16[512,256]{1,0:T(8,128)(2,1)S(1)} %copy-done), channel_id=1, source_target_pairs={{0,2},{1,3},{2,0},{3,1},{4,6},{5,7},{6,4},{7,5},{8,10},{9,11},{10,... | collective-permute-start | bytes 786440 | tf_op jit(solution)/shard_map/ppermute | solution.py:289
  7.5 0.7 copy-start.4
  8.3 5.6 %copy-start.2 = (s32[2]{0:T(128)S(1)}, s32[2]{0:T(128)}, u32[]{:S(2)}) copy-start(s32[2]{0:T(128)} %owner_ref.15) | copy-start | bytes 28
  39.5 34.3 %collective-permute-start.7 = (bf16[528,256]{1,0:T(8,128)(2,1)S(1)}, bf16[528,256]{1,0:T(8,128)(2,1)S(1)}, u32[]{:S(2)}, u32[]{:S(2)}) collective-permute-start(bf16[528,256]{1,0:T(8,128)(2,1)S(1)} %cross_last.7), channel_id=1, source_target_pairs={{0,3},{1,0},{2,1},{3,2},{4,7},{5,4},{6,5},{7,6},{8,11},{9,8},{10,9... | collective-permute-start | bytes 811016 | tf_op jit(solution)/shard_map/ppermute | solution.py:289
  47.6 26.1 %collective-permute-start.5 = (bf16[528,256]{1,0:T(8,128)(2,1)S(1)}, bf16[528,256]{1,0:T(8,128)(2,1)S(1)}, u32[]{:S(2)}, u32[]{:S(2)}) collective-permute-start(bf16[528,256]{1,0:T(8,128)(2,1)S(1)} %cross_last.6), channel_id=1, source_target_pairs={{0,1},{1,2},{2,3},{3,0},{4,5},{5,6},{6,7},{7,4},{8,9},{9,10},{10,1... | collective-permute-start | bytes 811016 | tf_op jit(solution)/shard_map/ppermute | solution.py:289
  54.6 19.1 %collective-permute-start.3 = (bf16[528,256]{1,0:T(8,128)(2,1)S(1)}, bf16[528,256]{1,0:T(8,128)(2,1)S(1)}, u32[]{:S(2)}, u32[]{:S(2)}) collective-permute-start(bf16[528,256]{1,0:T(8,128)(2,1)S(1)} %cross_last.5), channel_id=1, source_target_pairs={{0,2},{1,3},{2,0},{3,1},{4,6},{5,7},{6,4},{7,5},{8,10},{9,11},{10,... | collective-permute-start | bytes 811016 | tf_op jit(solution)/shard_map/ppermute | solution.py:289
  57.6 11.1 %collective-permute-start.1 = (bf16[512,256]{1,0:T(8,128)(2,1)S(1)}, bf16[512,256]{1,0:T(8,128)(2,1)S(1)}, u32[]{:S(2)}, u32[]{:S(2)}) collective-permute-start(bf16[512,256]{1,0:T(8,128)(2,1)S(1)} %bitcast.9), channel_id=1, source_target_pairs={{0,16},{1,17},{2,18},{3,19},{4,20},{5,21},{6,22},{7,23},{8,24},{9,... | collective-permute-start | bytes 786440 | tf_op jit(solution)/shard_map/ppermute | solution.py:323
  62.3 6.5 %copy-start.1 = (bf16[512,256]{1,0:T(8,128)(2,1)S(1)}, bf16[512,256]{1,0:T(8,128)(2,1)}, u32[]{:S(2)}) copy-start(bf16[512,256]{1,0:T(8,128)(2,1)} %q_ref.3) | copy-start | bytes 786436
where the time goes:
time: 75.5 us; the launch traced here: 75.3 us
  Pallas kernels  46 us (61%)
  waiting for transfers between devices  14.7 us (19%)
  starting transfers between devices  11.7 us (15%)
  local copies, waits for them, and re-layouts  2.22 us (3%)
    pallas_call x8, Pallas kernels, cross_part(): pl.pallas_call(functools.partial(cross_kernel, key_count, len(images), of...  39.3 us
    ppermute x7, waiting for transfers between devices, shifted(): lax.ppermute(value, axis, [(source, (source + steps) % count) for source...  14.7 us
    ppermute x7, starting transfers between devices, shifted(): lax.ppermute(value, axis, [(source, (source + steps) % count) for source...  10.4 us
    pallas_call x1, Pallas kernels, self_attention(): pl.pallas_call(functools.partial(self_kernel, pieces), out_shape=jax.Shap...  4.95 us
    unnamed x13, local copies, waits for them, and re-layouts  2.22 us
    pallas_call x1, Pallas kernels, combined(): pl.pallas_call(functools.partial(combine_kernel, len(parts)), out_shape=j...  1.52 us
  transfers between devices with their start and end apart: 8, of which 3 were waited for; matrix products, arithmetic and copies ran while one was open for 0% of the time, Pallas kernels for 50%

commit v1 on v0

v1 whole, which is shorter than its diff:
```python
import functools
import math

import jax
import jax.numpy as jnp
from jax import lax
from jax.experimental import pallas as pl
from jax.experimental.pallas import tpu as pltpu
from jax.sharding import PartitionSpec as P

HEAD_SIZE = 128
MASK_BLOCK_TOKENS = 128
LANES = 128
LOWEST = -1e30
MIXED_ROWS = HEAD_SIZE + 16
SHIFT_KEYS = 256
MOST_SUM = 2.0**100
LOG2_SCALE = math.log2(math.e) / math.sqrt(HEAD_SIZE)
VMEM_LIMIT = 48 * 1024 * 1024

VMEM = pl.BlockSpec(memory_space=pltpu.VMEM)
SMEM = pl.BlockSpec(memory_space=pltpu.SMEM)


def padded(count):
    return -(-count // LANES) * LANES


def nt_dot(a, b):
    return lax.dot_general(a, b, (((1,), (1,)), ((), ())), preferred_element_type=jnp.float32)


def at_block(block, size):
    return pl.ds(pl.multiple_of(block * size, size), size)


def stacked_heads(rows):
    heads = rows.shape[1] // HEAD_SIZE
    return jnp.concatenate([rows[:, h * HEAD_SIZE : (h + 1) * HEAD_SIZE] for h in range(heads)], axis=0)


def with_ones(value_t):
    shape = (MIXED_ROWS - HEAD_SIZE, value_t.shape[1])
    ones = (lax.broadcasted_iota(jnp.int32, shape, 0) == 0).astype(jnp.bfloat16)
    return jnp.concatenate([value_t, ones], axis=0)


def fold(high, mixed, scores, value_t, exact):
    seen = scores if exact else scores[0 : min(SHIFT_KEYS, scores.shape[0]), :]
    new_high = jnp.maximum(high, jnp.max(seen, axis=0, keepdims=True))
    weights = jnp.exp2(scores * LOG2_SCALE - new_high * LOG2_SCALE).astype(jnp.bfloat16)
    fading = jnp.exp2((high - new_high) * LOG2_SCALE)
    mixed = mixed * fading + jnp.dot(with_ones(value_t), weights, preferred_element_type=jnp.float32)
    return new_high, mixed


def prepare_kernel(kv_ref, out_ref):
    count = kv_ref.shape[1]
    whole = count // LANES * LANES
    rest = count - whole
    out_ref[0, 0:whole, :] = kv_ref[0, 0:whole, :]
    for at in range(0, whole, LANES):
        out_ref[1, at : at + LANES, :] = kv_ref[1, at : at + LANES, :].T
    if rest:
        empty = jnp.zeros((LANES - rest, HEAD_SIZE), jnp.float32)
        tail_key = jnp.concatenate([kv_ref[0, whole:count, :].astype(jnp.float32), empty], axis=0)
        tail_value = jnp.concatenate([kv_ref[1, whole:count, :].astype(jnp.float32), empty], axis=0)
        out_ref[0, whole : whole + LANES, :] = tail_key.astype(jnp.bfloat16)
        out_ref[1, whole : whole + LANES, :] = tail_value.T.astype(jnp.bfloat16)


def prepare(kv):
    return pl.pallas_call(
        prepare_kernel,
        out_shape=jax.ShapeDtypeStruct((2, padded(kv.shape[1]), HEAD_SIZE), jnp.bfloat16),
        in_specs=[VMEM],
        out_specs=VMEM,
        compiler_params=pltpu.CompilerParams(vmem_limit_bytes=VMEM_LIMIT),
        cost_estimate=pl.CostEstimate(flops=0, bytes_accessed=2 * kv.size * 2, transcendentals=0),
        name="prepare",
    )(kv)


def lse_rows(block_count):
    return -(-3 * block_count // 16) * 16


def cross_kernel(key_count, pieces, offset, last, position_ref, images_ref, owner_ref, q_ref, *refs):
    images, refs = refs[:pieces], refs[pieces:]
    if offset:
        before, refs = refs[:2], refs[2:]
    if last:
        out_ref, lse_ref, high_ref, mixed_ref, most_ref = refs
        lse_ref[...] = jnp.zeros_like(lse_ref)
    else:
        high_ref, mixed_ref, most_ref = refs
    slots = images_ref.shape[1]
    block_count = q_ref.shape[0] // MASK_BLOCK_TOKENS
    heads = q_ref.shape[1] // HEAD_SIZE
    rows = heads * MASK_BLOCK_TOKENS

    def attempt(exact):
        most_ref[...] = jnp.zeros_like(most_ref)

        def per_block(block, carry):
            here = 0 if last else block
            if offset:
                high_ref[here] = before[0][block]
                mixed_ref[here] = before[1][block]
            else:
                high_ref[here] = jnp.full(high_ref.shape[1:], LOWEST, jnp.float32)
                mixed_ref[here] = jnp.zeros(mixed_ref.shape[1:], jnp.float32)
            for piece in range(pieces):
                slot = lax.rem(position_ref[0] + (slots - offset - piece), slots)
                seen = jnp.int32(0)
                for image in range(slots):
                    seen = seen + jnp.where(owner_ref[image] == slot, images_ref[block, image], 0)

                @pl.when(seen > 0)
                def _(piece=piece):
                    image = images[piece]
                    width = image.shape[1]
                    queries = stacked_heads(q_ref[at_block(block, MASK_BLOCK_TOKENS), :])
                    scores = nt_dot(image[0], queries)
                    if width > key_count:
                        body = width - LANES
                        tail = scores[body:, :]
                        key_id = body + lax.broadcasted_iota(jnp.int32, tail.shape, 0)
                        tail = jnp.where(key_id < key_count, tail, LOWEST)
                        scores = jnp.concatenate([scores[:body, :], tail], axis=0) if body else tail
                    value_t = jnp.concatenate([image[1, c : c + LANES, :] for c in range(0, width, LANES)], axis=1)
                    high, mixed = fold(high_ref[here][0:1], mixed_ref[here], scores, value_t, exact)
                    high_ref[here] = jnp.broadcast_to(high, high_ref.shape[1:])
                    mixed_ref[here] = mixed

            total = mixed_ref[here][HEAD_SIZE : HEAD_SIZE + 1, :]
            most_ref[0:1, :] = jnp.maximum(most_ref[0:1, :], total)
            if last:
                out_ref[at_block(block, HEAD_SIZE), :] = (mixed_ref[here][0:HEAD_SIZE, :] / total).astype(jnp.bfloat16)
                lse = high_ref[here][0:1] * LOG2_SCALE + jnp.log2(total)
                row = lax.broadcasted_iota(jnp.int32, lse_ref.shape, 0)
                lse_ref[...] = jnp.where(row == block, lse, lse_ref[...])
            return carry

        lax.fori_loop(0, block_count, per_block, 0)

    attempt(False)
    fine = jnp.min((most_ref[0:1, :] <= MOST_SUM).astype(jnp.int32))

    @pl.when(fine == 0)
    def _():
        attempt(True)

    if last:
        lse = lse_ref[...]
        first = lse.astype(jnp.bfloat16).astype(jnp.float32)
        second = (lse - first).astype(jnp.bfloat16).astype(jnp.float32)
        third = lse - first - second
        parts = [part[0:block_count, :] for part in (first, second, third)]
        spare = lse_rows(block_count) - 3 * block_count
        if spare:
            parts.append(jnp.zeros((spare, rows), jnp.float32))
        out_ref[block_count * HEAD_SIZE :, :] = jnp.concatenate(parts, axis=0).astype(jnp.bfloat16)


def cross_part(tables, queries, images, key_count, offset, last, before=()):
    tokens, columns = queries.shape
    block_count = tokens // MASK_BLOCK_TOKENS
    rows = columns // HEAD_SIZE * MASK_BLOCK_TOKENS
    state = [(8, rows), (MIXED_ROWS, rows)]
    scratch = [pltpu.VMEM((8, rows), jnp.float32)]
    if last:
        out_shape = jax.ShapeDtypeStruct((block_count * HEAD_SIZE + lse_rows(block_count), rows), jnp.bfloat16)
        scratch = [pltpu.VMEM((1,) + shape, jnp.float32) for shape in state] + scratch
        scratch = [pltpu.VMEM((-(-block_count // 8) * 8, rows), jnp.float32)] + scratch
    else:
        out_shape = tuple(jax.ShapeDtypeStruct((block_count,) + shape, jnp.float32) for shape in state)
    flops = 4 * block_count * rows * key_count * HEAD_SIZE * len(images)
    return pl.pallas_call(
        functools.partial(cross_kernel, key_count, len(images), offset, last),
        out_shape=out_shape,
        in_specs=[SMEM, SMEM, SMEM] + [VMEM] * (1 + len(images) + len(before)),
        out_specs=VMEM if last else (VMEM,) * 2,
        scratch_shapes=scratch,
        compiler_params=pltpu.CompilerParams(vmem_limit_bytes=VMEM_LIMIT),
        cost_estimate=pl.CostEstimate(flops=2 * flops, bytes_accessed=4 * 1024 * 1024, transcendentals=0),
        name="cross_last" if last else "cross_first",
    )(*tables, queries, *images, *before)


def combine_kernel(parts, *refs):
    part_refs, out_ref = refs[:parts], refs[parts]
    tokens, columns = out_ref.shape
    block_count = tokens // MASK_BLOCK_TOKENS
    first_lse = block_count * HEAD_SIZE
    lse = []
    for ref in part_refs:
        tail = ref[first_lse:, :].astype(jnp.float32)
        lse.append(
            tail[0:block_count] + tail[block_count : 2 * block_count] + tail[2 * block_count : 3 * block_count]
        )
    highest = functools.reduce(jnp.maximum, lse)
    weights = [jnp.exp2(one - highest) for one in lse]
    total = functools.reduce(jnp.add, weights)
    weights = [one / total for one in weights]
    for block in range(block_count):
        mixed = 0.0
        for ref, weight in zip(part_refs, weights):
            part = ref[block * HEAD_SIZE : (block + 1) * HEAD_SIZE, :].astype(jnp.float32)
            mixed = mixed + weight[block : block + 1, :] * part
        store_heads(out_ref, block, mixed)


def store_heads(out_ref, block, mixed):
    at = slice(block * MASK_BLOCK_TOKENS, (block + 1) * MASK_BLOCK_TOKENS)
    for head in range(out_ref.shape[1] // HEAD_SIZE):
        piece = mixed[:, head * MASK_BLOCK_TOKENS : (head + 1) * MASK_BLOCK_TOKENS]
        out_ref[at, head * HEAD_SIZE : (head + 1) * HEAD_SIZE] = piece.T.astype(jnp.bfloat16)


def combined(parts, shape):
    return pl.pallas_call(
        functools.partial(combine_kernel, len(parts)),
        out_shape=jax.ShapeDtypeStruct(shape, jnp.bfloat16),
        in_specs=[VMEM] * len(parts),
        out_specs=VMEM,
        compiler_params=pltpu.CompilerParams(vmem_limit_bytes=VMEM_LIMIT),
        cost_estimate=pl.CostEstimate(flops=0, bytes_accessed=2 * 1024 * 1024, transcendentals=0),
        name="combine",
    )(*parts)


def self_kernel(pieces, position_ref, q_ref, *refs):
    texts = refs[:pieces]
    out_ref, value_ref, high_ref, mixed_ref = refs[pieces:]
    tokens, columns = q_ref.shape
    rows = columns // HEAD_SIZE * MASK_BLOCK_TOKENS
    value_ref[0] = texts[0][:, HEAD_SIZE:].T
    for piece in range(1, pieces):

        @pl.when(position_ref[0] >= piece)
        def _(piece=piece):
            value_ref[piece] = texts[piece][:, HEAD_SIZE:].T

    for block in range(tokens // MASK_BLOCK_TOKENS):
        start = block * MASK_BLOCK_TOKENS
        stop = start + MASK_BLOCK_TOKENS
        queries = stacked_heads(q_ref[start:stop, :])
        scores = nt_dot(texts[0][0:stop, 0:HEAD_SIZE], queries)
        tail = scores[start:, :]
        key_id = lax.broadcasted_iota(jnp.int32, tail.shape, 0)
        query_id = lax.broadcasted_iota(jnp.int32, tail.shape, 1) % MASK_BLOCK_TOKENS
        tail = jnp.where(key_id <= query_id, tail, LOWEST)
        scores = jnp.concatenate([scores[:start, :], tail], axis=0) if start else tail
        high = jnp.full((1, rows), LOWEST, jnp.float32)
        mixed = jnp.zeros((MIXED_ROWS, rows), jnp.float32)
        high, mixed = fold(high, mixed, scores, value_ref[0, :, 0:stop], True)
        high_ref[0:1, :] = high
        mixed_ref[...] = mixed
        for piece in range(1, pieces):

            @pl.when(position_ref[0] >= piece)
            def _(piece=piece):
                scores = nt_dot(texts[piece][:, 0:HEAD_SIZE], queries)
                high, mixed = fold(high_ref[0:1, :], mixed_ref[...], scores, value_ref[piece], True)
                high_ref[0:1, :] = high
                mixed_ref[...] = mixed

        store_heads(out_ref, block, mixed_ref[0:HEAD_SIZE, :] / mixed_ref[HEAD_SIZE : HEAD_SIZE + 1, :])


def self_attention(position, queries, texts):
    tokens, columns = queries.shape
    pieces = len(texts)
    rows = columns // HEAD_SIZE * MASK_BLOCK_TOKENS
    return pl.pallas_call(
        functools.partial(self_kernel, pieces),
        out_shape=jax.ShapeDtypeStruct((tokens, columns), jnp.bfloat16),
        in_specs=[SMEM] + [VMEM] * (1 + pieces),
        out_specs=VMEM,
        scratch_shapes=[
            pltpu.VMEM((pieces, HEAD_SIZE, tokens), jnp.bfloat16),
            pltpu.VMEM((8, rows), jnp.float32),
            pltpu.VMEM((MIXED_ROWS, rows), jnp.float32),
        ],
        compiler_params=pltpu.CompilerParams(vmem_limit_bytes=VMEM_LIMIT),
        cost_estimate=pl.CostEstimate(flops=8 * tokens * columns * tokens, bytes_accessed=1024 * 1024, transcendentals=0),
        name="self_attention",
    )(position, queries, *texts)


def shifted(value, axis, steps):
    count = lax.axis_size(axis)
    return lax.ppermute(value, axis, [(source, (source + steps) % count) for source in range(count)])


def per_device(self_queries, text_kv, cross_queries, image_kv, block_images, image_owner):
    rows = self_queries.shape[0]
    key_count = image_kv.shape[2]
    cycle = lax.axis_size("blk")
    ring = lax.axis_size("enc")
    position = lax.axis_index("blk").astype(jnp.int32)[None]

    tables = (position, block_images, image_owner)

    images = [prepare(image_kv[0])]
    for _ in range(1, cycle):
        images.append(shifted(images[-1], "blk", 1))
    order = sorted(range(1, ring), key=lambda step: (abs(2 * step - ring), step))
    queries = {step: shifted(cross_queries, "enc", ring - step) for step in order}
    queries[0] = cross_queries

    text = text_kv.reshape(rows, 2 * HEAD_SIZE)
    texts = [text]
    for step in range(1, cycle):
        texts.append(lax.ppermute(texts[-1], "blk", [(source, source + 1) for source in range(cycle - 1)]))

    alone = cycle == 1
    states = {0: ()}
    if not alone:
        states[0] = cross_part(tables, queries[0], images[:1], key_count, 0, False)
    earlier = states[0]
    for step in order:
        if alone:
            states[step] = ()
        else:
            queries[step], _ = lax.optimization_barrier((queries[step], earlier))
            earlier = states[step] = cross_part(tables, queries[step], images[:1], key_count, 0, False)

    def finished(step):
        offset = 0 if alone else 1
        return cross_part(tables, queries[step], images[offset:], key_count, offset, True, states[step])

    received = [shifted(finished(step), "enc", step) for step in order]

    own = finished(0)
    self_out = self_attention(position, self_queries, texts)
    cross_out = combined([own] + received, cross_queries.shape)
    return (self_out, cross_out)


def solution(mesh):
    placed = (
        P("blk", ("tp", "enc")),
        P("blk", None, "tp"),
        P("blk", ("tp", "enc")),
        P("blk", None, "enc", "tp"),
        P("blk", None),
        P(),
    )
    return jax.shard_map(
        per_device,
        mesh=mesh,
        in_specs=placed,
        out_specs=(P("blk", ("tp", "enc")), P("blk", ("tp", "enc"))),
        check_vma=False,
    )
```

time: 75.5 us -> 63.9 us (0.85)
  the two profiles are of different devices: /device:TPU:6 before, /device:TPU:0 now
where the time goes in v1:
time: 63.9 us; the launch traced here: 64.4 us
  Pallas kernels  29.5 us (46%)
  waiting for transfers between devices  17.1 us (27%)
  starting transfers between devices  14.3 us (22%)
  local copies, waits for them, and re-layouts  2.73 us (4%)
  between operations  0.76 us (1%)
    pallas_call x8, Pallas kernels, cross_part(): pl.pallas_call(functools.partial(cross_kernel, key_count, len(images), of...  25.3 us
    ppermute x7, waiting for transfers between devices, shifted(): lax.ppermute(value, axis, [(source, (source + steps) % count) for source...  17.1 us
    ppermute x7, starting transfers between devices, shifted(): lax.ppermute(value, axis, [(source, (source + steps) % count) for source...  11.7 us
    pallas_call x1, Pallas kernels, self_attention(): pl.pallas_call(functools.partial(self_kernel, pieces), out_shape=jax.Shap...  3.05 us
    unnamed x13, local copies, waits for them, and re-layouts  2.73 us
    ppermute x1, starting transfers between devices, per_device(): lax.ppermute(texts[-1], 'blk', [(source, source + 1) for source in range(...  2.59 us
  transfers between devices with their start and end apart: 8, of which 3 were waited for; matrix products, arithmetic and copies ran while one was open for 0% of the time, Pallas kernels for 44%

profile of v1, /device:TPU:0, one launch (start us, length us, event | category | flops | bytes accessed | tf_op | source)
XLA Modules:
  0.0 64.4 jit_solution(7863140121503609432)
XLA Ops:
  0.6 1.3 %copy.20 = bf16[1,2,1601,128]{3,2,1,0:T(8,128)(2,1)S(1)} copy(bf16[1,2,1601,128]{3,1,2,0:T(2,128)(2,1)} %param.9) | data formatting | bytes 1639424 | tf_op args[3]
  1.9 0.0 copy-start.1
  1.9 0.0 copy-start.3
  1.9 0.2 prepare.1.refs_0_
  2.1 3.0 %collective-permute-start.1 = (bf16[2,1664,128]{2,1,0:T(8,128)(2,1)S(1)}, bf16[2,1664,128]{2,1,0:T(8,128)(2,1)S(1)}, u32[]{:S(2)}, u32[]{:S(2)}) collective-permute-start(bf16[2,1664,128]{2,1,0:T(8,128)(2,1)S(1)} %prepare.1.refs_0_), channel_id=1, source_target_pairs={{0,16},{16,0},{1,17},{17,1},{2,18},{18,2},{3,19},{19,3},{4,20},{20... | collective-permute-start | bytes 2555912 | tf_op jit(solution)/shard_map/ppermute | solution.py:294
  5.1 0.0 copy-done.1
  5.1 2.6 %collective-permute-start.2 = (bf16[512,256]{1,0:T(8,128)(2,1)S(1)}, bf16[512,256]{1,0:T(8,128)(2,1)S(1)}, u32[]{:S(2)}, u32[]{:S(2)}) collective-permute-start(bf16[512,256]{1,0:T(8,128)(2,1)S(1)} %copy-done.1), channel_id=1, source_target_pairs={{0,2},{1,3},{2,0},{3,1},{4,6},{5,7},{6,4},{7,5},{8,10},{9,11},{10,... | collective-permute-start | bytes 786440 | tf_op jit(solution)/shard_map/ppermute | solution.py:294
  7.7 1.3 %collective-permute-start.4 = (bf16[512,256]{1,0:T(8,128)(2,1)S(1)}, bf16[512,256]{1,0:T(8,128)(2,1)S(1)}, u32[]{:S(2)}, u32[]{:S(2)}) collective-permute-start(bf16[512,256]{1,0:T(8,128)(2,1)S(1)} %copy-done.1), channel_id=1, source_target_pairs={{0,3},{1,0},{2,1},{3,2},{4,7},{5,4},{6,5},{7,6},{8,11},{9,8},{10,9... | collective-permute-start | bytes 786440 | tf_op jit(solution)/shard_map/ppermute | solution.py:294
  9.0 0.7 %collective-permute-start.6 = (bf16[512,256]{1,0:T(8,128)(2,1)S(1)}, bf16[512,256]{1,0:T(8,128)(2,1)S(1)}, u32[]{:S(2)}, u32[]{:S(2)}) collective-permute-start(bf16[512,256]{1,0:T(8,128)(2,1)S(1)} %copy-done.1), channel_id=1, source_target_pairs={{0,1},{1,2},{2,3},{3,0},{4,5},{5,6},{6,7},{7,4},{8,9},{9,10},{10,1... | collective-permute-start | bytes 786440 | tf_op jit(solution)/shard_map/ppermute | solution.py:294
  9.7 0.0 copy-done.3
  9.8 2.6 %collective-permute-start = (bf16[512,256]{1,0:T(8,128)(2,1)S(1)}, bf16[512,256]{1,0:T(8,128)(2,1)S(1)}, u32[]{:S(2)}, u32[]{:S(2)}) collective-permute-start(bf16[512,256]{1,0:T(8,128)(2,1)S(1)} %bitcast.9), channel_id=1, source_target_pairs={{0,16},{1,17},{2,18},{3,19},{4,20},{5,21},{6,22},{7,23},{8,24},{9,... | collective-permute-start | bytes 786440 | tf_op jit(solution)/shard_map/ppermute | solution.py:316
  12.4 0.0 copy-start.4
  12.4 0.7 %copy-done.4 = s32[4,2]{0,1:T(2,128)S(1)} copy-done((s32[4,2]{0,1:T(2,128)S(1)}, s32[4,2]{0,1:T(2,128)}, u32[]{:S(2)}) %copy-start.4) | copy-done | bytes 56
  13.1 0.1 copy.10.images_ref
  13.1 0.0 copy-start.2
  13.1 0.7 %copy-done.2 = s32[2]{0:T(128)S(1)} copy-done((s32[2]{0:T(128)S(1)}, s32[2]{0:T(128)}, u32[]{:S(2)}) %copy-start.2) | copy-done | bytes 32
  13.8 3.9 %cross_first.4 = (f32[4,8,256]{2,1,0:T(8,128)S(1)}, f32[4,144,256]{2,1,0:T(8,128)S(1)}) custom-call(s32[1]{0:T(128)} %bitcast.position_ref, s32[4,2]{1,0:T(4,128)S(1)} %copy.10.images_ref, s32[2]{0:T(128)S(1)} %copy-done.2, bf16[512,256]{1,0:T(8,128)(2,1)S(1)} %copy-done.1, bf16[2,1664,128]{2,1,0:T(8,128)(2,1)S(1)} %prepare.1.refs_0_), custom_call_target="tpu_custom_call" | custom-call | flops 1678770176 | bytes 4194304 | tf_op jit(solution)/shard_map/cross_first/pallas_call | solution.py:179
  17.7 8.5 %collective-permute-done.2.q_ref = bf16[512,256]{1,0:T(8,128)(2,1)S(1)} collective-permute-done((bf16[512,256]{1,0:T(8,128)(2,1)S(1)}, bf16[512,256]{1,0:T(8,128)(2,1)S(1)}, u32[]{:S(2)}, u32[]{:S(2)}) %collective-permute-start.2) | collective-permute-done | bytes 262176 | tf_op jit(solution)/shard_map/ppermute | solution.py:294
  26.2 3.9 %cross_first.5 = (f32[4,8,256]{2,1,0:T(8,128)S(1)}, f32[4,144,256]{2,1,0:T(8,128)S(1)}) custom-call(s32[1]{0:T(128)} %bitcast.position_ref, s32[4,2]{1,0:T(4,128)S(1)} %copy.10.images_ref, s32[2]{0:T(128)S(1)} %copy-done.2, bf16[512,256]{1,0:T(8,128)(2,1)S(1)} %collective-permute-done.2.q_ref, bf16[2,1664,128]{2,1,0:T(8,128)(2,1)S(1)} %prepare.1.refs_0_), custom_call_target="tpu_custom_call" | custom-call | flops 1678770176 | bytes 4194304 | tf_op jit(solution)/shard_map/cross_first/pallas_call | solution.py:179
  30.1 0.0 collective-permute-done.4.q_ref
  30.1 3.9 %cross_first.6 = (f32[4,8,256]{2,1,0:T(8,128)S(1)}, f32[4,144,256]{2,1,0:T(8,128)S(1)}) custom-call(s32[1]{0:T(128)} %bitcast.position_ref, s32[4,2]{1,0:T(4,128)S(1)} %copy.10.images_ref, s32[2]{0:T(128)S(1)} %copy-done.2, bf16[512,256]{1,0:T(8,128)(2,1)S(1)} %collective-permute-done.4.q_ref, bf16[2,1664,128]{2,1,0:T(8,128)(2,1)S(1)} %prepare.1.refs_0_), custom_call_target="tpu_custom_call" | custom-call | flops 1678770176 | bytes 4194304 | tf_op jit(solution)/shard_map/cross_first/pallas_call | solution.py:179
  34.0 0.0 collective-permute-done.6.q_ref
  34.1 3.9 %cross_first.7 = (f32[4,8,256]{2,1,0:T(8,128)S(1)}, f32[4,144,256]{2,1,0:T(8,128)S(1)}) custom-call(s32[1]{0:T(128)} %bitcast.position_ref, s32[4,2]{1,0:T(4,128)S(1)} %copy.10.images_ref, s32[2]{0:T(128)S(1)} %copy-done.2, bf16[512,256]{1,0:T(8,128)(2,1)S(1)} %collective-permute-done.6.q_ref, bf16[2,1664,128]{2,1,0:T(8,128)(2,1)S(1)} %prepare.1.refs_0_), custom_call_target="tpu_custom_call" | custom-call | flops 1678770176 | bytes 4194304 | tf_op jit(solution)/shard_map/cross_first/pallas_call | solution.py:179
  38.0 0.0 collective-permute-done.1.refs_0_
  38.0 2.4 %cross_last.5 = bf16[528,256]{1,0:T(8,128)(2,1)S(1)} custom-call(s32[1]{0:T(128)} %bitcast.position_ref, s32[4,2]{1,0:T(4,128)S(1)} %copy.10.images_ref, s32[2]{0:T(128)S(1)} %copy-done.2, bf16[512,256]{1,0:T(8,128)(2,1)S(1)} %collective-permute-done.2.q_ref, bf16[2,1664,128]{2,1,0:T(8,128)(2,1)S(1)} %collective-permute-done.1.refs_0_, ...), custom_call_target="tpu_custom_call" | custom-call | flops 1678770176 | bytes 4194304 | tf_op jit(solution)/shard_map/cross_last/pallas_call | solution.py:179
  40.4 0.2 collective-permute-start.3
  40.6 2.4 %cross_last.6 = bf16[528,256]{1,0:T(8,128)(2,1)S(1)} custom-call(s32[1]{0:T(128)} %bitcast.position_ref, s32[4,2]{1,0:T(4,128)S(1)} %copy.10.images_ref, s32[2]{0:T(128)S(1)} %copy-done.2, bf16[512,256]{1,0:T(8,128)(2,1)S(1)} %collective-permute-done.4.q_ref, bf16[2,1664,128]{2,1,0:T(8,128)(2,1)S(1)} %collective-permute-done.1.refs_0_, ...), custom_call_target="tpu_custom_call" | custom-call | flops 1678770176 | bytes 4194304 | tf_op jit(solution)/shard_map/cross_last/pallas_call | solution.py:179
  43.0 3.0 %collective-permute-start.5 = (bf16[528,256]{1,0:T(8,128)(2,1)S(1)}, bf16[528,256]{1,0:T(8,128)(2,1)S(1)}, u32[]{:S(2)}, u32[]{:S(2)}) collective-permute-start(bf16[528,256]{1,0:T(8,128)(2,1)S(1)} %cross_last.6), channel_id=1, source_target_pairs={{0,1},{1,2},{2,3},{3,0},{4,5},{5,6},{6,7},{7,4},{8,9},{9,10},{10,1... | collective-permute-start | bytes 811016 | tf_op jit(solution)/shard_map/ppermute | solution.py:294
  46.0 0.0 copy-start
  46.0 2.4 %cross_last.7 = bf16[528,256]{1,0:T(8,128)(2,1)S(1)} custom-call(s32[1]{0:T(128)} %bitcast.position_ref, s32[4,2]{1,0:T(4,128)S(1)} %copy.10.images_ref, s32[2]{0:T(128)S(1)} %copy-done.2, bf16[512,256]{1,0:T(8,128)(2,1)S(1)} %collective-permute-done.6.q_ref, bf16[2,1664,128]{2,1,0:T(8,128)(2,1)S(1)} %collective-permute-done.1.refs_0_, ...), custom_call_target="tpu_custom_call" | custom-call | flops 1678770176 | bytes 4194304 | tf_op jit(solution)/shard_map/cross_last/pallas_call | solution.py:179
  48.4 1.0 %collective-permute-start.7 = (bf16[528,256]{1,0:T(8,128)(2,1)S(1)}, bf16[528,256]{1,0:T(8,128)(2,1)S(1)}, u32[]{:S(2)}, u32[]{:S(2)}) collective-permute-start(bf16[528,256]{1,0:T(8,128)(2,1)S(1)} %cross_last.7), channel_id=1, source_target_pairs={{0,3},{1,0},{2,1},{3,2},{4,7},{5,4},{6,5},{7,6},{8,11},{9,8},{10,9... | collective-permute-start | bytes 811016 | tf_op jit(solution)/shard_map/ppermute | solution.py:294
  49.4 0.0 collective-permute-done.refs_1_
  49.4 0.0 copy-done
  49.4 3.0 %self_attention.1 = bf16[512,256]{1,0:T(8,128)(2,1)} custom-call(s32[1]{0:T(128)} %bitcast.position_ref, bf16[512,256]{1,0:T(8,128)(2,1)S(1)} %copy-done, bf16[512,256]{1,0:T(8,128)(2,1)S(1)} %bitcast.10, bf16[512,256]{1,0:T(8,128)(2,1)S(1)} %collective-permute-done.refs_1_), custom_call_target="tpu_custom_call" | custom-call | flops 536870912 | bytes 1048576 | tf_op jit(solution)/shard_map/self_attention/pallas_call | solution.py:276
  52.4 2.4 %cross_last.4.refs_0_ = bf16[528,256]{1,0:T(8,128)(2,1)S(1)} custom-call(s32[1]{0:T(128)} %bitcast.position_ref, s32[4,2]{1,0:T(4,128)S(1)} %copy.10.images_ref, s32[2]{0:T(128)S(1)} %copy-done.2, bf16[512,256]{1,0:T(8,128)(2,1)S(1)} %copy-done.1, bf16[2,1664,128]{2,1,0:T(8,128)(2,1)S(1)} %collective-permute-done.1.refs_0_, ...), custom_call_target="tpu_custom_call" | custom-call | flops 1678770176 | bytes 4194304 | tf_op jit(solution)/shard_map/cross_last/pallas_call | solution.py:179
  54.8 6.2 %collective-permute-done.3.refs_1_ = bf16[528,256]{1,0:T(8,128)(2,1)S(1)} collective-permute-done((bf16[528,256]{1,0:T(8,128)(2,1)S(1)}, bf16[528,256]{1,0:T(8,128)(2,1)S(1)}, u32[]{:S(2)}, u32[]{:S(2)}) %collective-permute-start.3) | collective-permute-done | bytes 270368 | tf_op jit(solution)/shard_map/ppermute | solution.py:294
  61.0 0.0 collective-permute-done.5.refs_2_
  61.0 2.4 %collective-permute-done.7.refs_3_ = bf16[528,256]{1,0:T(8,128)(2,1)S(1)} collective-permute-done((bf16[528,256]{1,0:T(8,128)(2,1)S(1)}, bf16[528,256]{1,0:T(8,128)(2,1)S(1)}, u32[]{:S(2)}, u32[]{:S(2)}) %collective-permute-start.7) | collective-permute-done | bytes 270368 | tf_op jit(solution)/shard_map/ppermute | solution.py:294
  63.4 1.0 %combine.1 = bf16[512,256]{1,0:T(8,128)(2,1)} custom-call(bf16[528,256]{1,0:T(8,128)(2,1)S(1)} %cross_last.4.refs_0_, bf16[528,256]{1,0:T(8,128)(2,1)S(1)} %collective-permute-done.3.refs_1_, bf16[528,256]{1,0:T(8,128)(2,1)S(1)} %collective-permute-done.5.refs_2_, bf16[528,256]{1,0:T(8,128)(2,1)S(1)} %collective-permute-done.7.refs_3_), custom_call_target="tpu_custom_call" | custom-call | bytes 2097152 | tf_op jit(solution)/shard_map/combine/pallas_call | solution.py:222
  (1 shorter events, 0.0 us)
Async XLA Ops:
  1.9 3.2 %copy-start.1 = (bf16[512,256]{1,0:T(8,128)(2,1)S(1)}, bf16[512,256]{1,0:T(8,128)(2,1)}, u32[]{:S(2)}) copy-start(bf16[512,256]{1,0:T(8,128)(2,1)} %q_ref.5) | copy-start | bytes 786436
  1.9 7.8 %copy-start.3 = (bf16[512,2,128]{2,1,0:T(2,128)(2,1)S(1)}, bf16[512,2,128]{2,1,0:T(2,128)(2,1)}, u32[]{:S(2)}) copy-start(bf16[512,2,128]{2,1,0:T(2,128)(2,1)} %param.7) | copy-start | bytes 786436
  2.1 35.9 %collective-permute-start.1 = (bf16[2,1664,128]{2,1,0:T(8,128)(2,1)S(1)}, bf16[2,1664,128]{2,1,0:T(8,128)(2,1)S(1)}, u32[]{:S(2)}, u32[]{:S(2)}) collective-permute-start(bf16[2,1664,128]{2,1,0:T(8,128)(2,1)S(1)} %prepare.1.refs_0_), channel_id=1, source_target_pairs={{0,16},{16,0},{1,17},{17,1},{2,18},{18,2},{3,19},{19,3},{4,20},{20... | collective-permute-start | bytes 2555912 | tf_op jit(solution)/shard_map/ppermute | solution.py:294
  5.1 21.1 %collective-permute-start.2 = (bf16[512,256]{1,0:T(8,128)(2,1)S(1)}, bf16[512,256]{1,0:T(8,128)(2,1)S(1)}, u32[]{:S(2)}, u32[]{:S(2)}) collective-permute-start(bf16[512,256]{1,0:T(8,128)(2,1)S(1)} %copy-done.1), channel_id=1, source_target_pairs={{0,2},{1,3},{2,0},{3,1},{4,6},{5,7},{6,4},{7,5},{8,10},{9,11},{10,... | collective-permute-start | bytes 786440 | tf_op jit(solution)/shard_map/ppermute | solution.py:294
  7.7 22.4 %collective-permute-start.4 = (bf16[512,256]{1,0:T(8,128)(2,1)S(1)}, bf16[512,256]{1,0:T(8,128)(2,1)S(1)}, u32[]{:S(2)}, u32[]{:S(2)}) collective-permute-start(bf16[512,256]{1,0:T(8,128)(2,1)S(1)} %copy-done.1), channel_id=1, source_target_pairs={{0,3},{1,0},{2,1},{3,2},{4,7},{5,4},{6,5},{7,6},{8,11},{9,8},{10,9... | collective-permute-start | bytes 786440 | tf_op jit(solution)/shard_map/ppermute | solution.py:294
  9.0 25.0 %collective-permute-start.6 = (bf16[512,256]{1,0:T(8,128)(2,1)S(1)}, bf16[512,256]{1,0:T(8,128)(2,1)S(1)}, u32[]{:S(2)}, u32[]{:S(2)}) collective-permute-start(bf16[512,256]{1,0:T(8,128)(2,1)S(1)} %copy-done.1), channel_id=1, source_target_pairs={{0,1},{1,2},{2,3},{3,0},{4,5},{5,6},{6,7},{7,4},{8,9},{9,10},{10,1... | collective-permute-start | bytes 786440 | tf_op jit(solution)/shard_map/ppermute | solution.py:294
  9.8 39.6 %collective-permute-start = (bf16[512,256]{1,0:T(8,128)(2,1)S(1)}, bf16[512,256]{1,0:T(8,128)(2,1)S(1)}, u32[]{:S(2)}, u32[]{:S(2)}) collective-permute-start(bf16[512,256]{1,0:T(8,128)(2,1)S(1)} %bitcast.9), channel_id=1, source_target_pairs={{0,16},{1,17},{2,18},{3,19},{4,20},{5,21},{6,22},{7,23},{8,24},{9,... | collective-permute-start | bytes 786440 | tf_op jit(solution)/shard_map/ppermute | solution.py:316
  12.4 0.7 %copy-start.4 = (s32[4,2]{0,1:T(2,128)S(1)}, s32[4,2]{0,1:T(2,128)}, u32[]{:S(2)}) copy-start(s32[4,2]{0,1:T(2,128)} %param.10) | copy-start | bytes 100
  13.1 0.7 %copy-start.2 = (s32[2]{0:T(128)S(1)}, s32[2]{0:T(128)}, u32[]{:S(2)}) copy-start(s32[2]{0:T(128)} %owner_ref.15) | copy-start | bytes 28
  40.4 20.6 %collective-permute-start.3 = (bf16[528,256]{1,0:T(8,128)(2,1)S(1)}, bf16[528,256]{1,0:T(8,128)(2,1)S(1)}, u32[]{:S(2)}, u32[]{:S(2)}) collective-permute-start(bf16[528,256]{1,0:T(8,128)(2,1)S(1)} %cross_last.5), channel_id=1, source_target_pairs={{0,2},{1,3},{2,0},{3,1},{4,6},{5,7},{6,4},{7,5},{8,10},{9,11},{10,... | collective-permute-start | bytes 811016 | tf_op jit(solution)/shard_map/ppermute | solution.py:294
  43.0 18.0 %collective-permute-start.5 = (bf16[528,256]{1,0:T(8,128)(2,1)S(1)}, bf16[528,256]{1,0:T(8,128)(2,1)S(1)}, u32[]{:S(2)}, u32[]{:S(2)}) collective-permute-start(bf16[528,256]{1,0:T(8,128)(2,1)S(1)} %cross_last.6), channel_id=1, source_target_pairs={{0,1},{1,2},{2,3},{3,0},{4,5},{5,6},{6,7},{7,4},{8,9},{9,10},{10,1... | collective-permute-start | bytes 811016 | tf_op jit(solution)/shard_map/ppermute | solution.py:294
  46.0 3.4 %copy-start = (bf16[512,256]{1,0:T(8,128)(2,1)S(1)}, bf16[512,256]{1,0:T(8,128)(2,1)}, u32[]{:S(2)}) copy-start(bf16[512,256]{1,0:T(8,128)(2,1)} %q_ref.3) | copy-start | bytes 786436
  48.4 15.1 %collective-permute-start.7 = (bf16[528,256]{1,0:T(8,128)(2,1)S(1)}, bf16[528,256]{1,0:T(8,128)(2,1)S(1)}, u32[]{:S(2)}, u32[]{:S(2)}) collective-permute-start(bf16[528,256]{1,0:T(8,128)(2,1)S(1)} %cross_last.7), channel_id=1, source_target_pairs={{0,3},{1,0},{2,1},{3,2},{4,7},{5,4},{6,5},{7,6},{8,11},{9,8},{10,9... | collective-permute-start | bytes 811016 | tf_op jit(solution)/shard_map/ppermute | solution.py:294

commit v2 on v0

--- a/solution.py
+++ b/solution.py
@@ -12,6 +12,9 @@
 MASK_BLOCK_TOKENS = 128
 LANES = 128
 LOWEST = -1e30
+SHIFT_KEYS = 256
+CHUNK = 512
+MOST_SUM = 2.0**100
 LOG2_SCALE = math.log2(math.e) / math.sqrt(HEAD_SIZE)
 VMEM_LIMIT = 48 * 1024 * 1024
 
@@ -27,8 +30,8 @@
     return lax.dot_general(a, b, (((1,), (1,)), ((), ())), preferred_element_type=jnp.float32)
 
 
-def at_block(block):
-    return pl.ds(pl.multiple_of(block * MASK_BLOCK_TOKENS, MASK_BLOCK_TOKENS), MASK_BLOCK_TOKENS)
+def at_block(block, size=MASK_BLOCK_TOKENS):
+    return pl.ds(pl.multiple_of(block * size, size), size)
 
 
 def stacked_heads(rows):
@@ -40,22 +43,41 @@
     return [wide[:, at : at + LANES] for at in range(0, wide.shape[1], LANES)]
 
 
+def row_max(scores):
+    return jnp.max(functools.reduce(jnp.maximum, lane_tiles(scores)), axis=1, keepdims=True)
+
+
 def empty_state(rows):
     return (
-        jnp.full((rows, 1), LOWEST, jnp.float32),
+        jnp.full((rows, LANES), LOWEST, jnp.float32),
         jnp.zeros((rows, LANES), jnp.float32),
         jnp.zeros((rows, HEAD_SIZE), jnp.float32),
     )
 
 
-def fold(state, scores, value):
+def fold_chunks(state, chunks, scores_of, values_of, exact):
     high, total, mixed = state
-    new_high = jnp.maximum(high, jnp.max(functools.reduce(jnp.maximum, lane_tiles(scores)), axis=1, keepdims=True))
-    weights = jnp.exp2(scores * LOG2_SCALE - new_high * LOG2_SCALE)
+    scores = scores_of(chunks[0])
+    seen = row_max(scores[:, 0 : min(SHIFT_KEYS, scores.shape[1])])
+    if exact:
+        seen = functools.reduce(jnp.maximum, [row_max(scores_of(chunk)) for chunk in chunks])
+    new_high = jnp.maximum(high, seen)
+    shift = new_high * LOG2_SCALE
     fading = jnp.exp2((high - new_high) * LOG2_SCALE)
-    total = total * fading + functools.reduce(jnp.add, lane_tiles(weights))
-    mixed = mixed * fading + jnp.dot(weights.astype(jnp.bfloat16), value, preferred_element_type=jnp.float32)
-    return (new_high, total, mixed)
+    total = total * fading
+    mixed = mixed * fading
+    waiting = None
+    for index, chunk in enumerate(chunks):
+        following = scores_of(chunks[index + 1]) if index + 1 < len(chunks) else None
+        weights = [jnp.exp2(tile * LOG2_SCALE - shift) for tile in lane_tiles(scores)]
+        total = total + functools.reduce(jnp.add, weights)
+        if waiting is not None:
+            mixed = mixed + jnp.dot(*waiting, preferred_element_type=jnp.float32)
+        weights = [tile.astype(jnp.bfloat16) for tile in weights]
+        waiting = (jnp.concatenate(weights, axis=1) if len(weights) > 1 else weights[0], values_of(chunk))
+        scores = following
+    mixed = mixed + jnp.dot(*waiting, preferred_element_type=jnp.float32)
+    return new_high, total, mixed
 
 
 def prepare_kernel(kv_ref, out_ref):
@@ -85,13 +107,13 @@
     )(kv)
 
 
-def chunk_starts(width):
-    half = width // LANES // 2 * LANES
-    return [(0, half), (half, width)] if half else [(0, width)]
-
-
 def lse_rows(block_count):
     return -(-3 * block_count // 16) * 16
+
+
+def chunks_of(width):
+    starts = list(range(0, max(width - CHUNK // 2, 1), CHUNK))
+    return list(zip(starts, starts[1:] + [width]))
 
 
 def cross_kernel(key_count, pieces, offset, last, position_ref, images_ref, owner_ref, q_ref, *refs):
@@ -99,61 +121,80 @@
     if offset:
         before, refs = refs[:3], refs[3:]
     if last:
-        out_ref, lse_ref = refs[0], refs[1]
-        state_refs = refs[2:]
-        lse_ref[...] = jnp.zeros_like(lse_ref)
+        out_ref, lse_ref, list_ref, *state_refs = refs
     else:
-        state_refs = refs
+        *state_refs, list_ref = refs
     slots = images_ref.shape[1]
     block_count = q_ref.shape[0] // MASK_BLOCK_TOKENS
     heads = q_ref.shape[1] // HEAD_SIZE
     rows = heads * MASK_BLOCK_TOKENS
 
-    def per_block(block, carry):
-        at = pl.ds(pl.multiple_of(block * rows, rows), rows)
-        here = at if not last else slice(None)
-        if offset:
-            for ref, old in zip(state_refs, before):
-                ref[here, :] = old[at, :]
-        else:
-            for ref, value in zip(state_refs, empty_state(rows)):
-                ref[here, :] = jnp.broadcast_to(value, (rows, LANES))
+    def attempt(exact):
+        for block in range(block_count):
+            at = slice(block * rows, (block + 1) * rows)
+            for index, value in enumerate(empty_state(rows)):
+                state_refs[index][at, :] = before[index][at, :] if offset else value
         for piece in range(pieces):
             slot = lax.rem(position_ref[0] + (slots - offset - piece), slots)
-            seen = jnp.int32(0)
-            for image in range(slots):
-                seen = seen + jnp.where(owner_ref[image] == slot, images_ref[block, image], 0)
-
-            @pl.when(seen > 0)
-            def _(piece=piece):
+
+            def collect(block, count):
+                seen = jnp.int32(0)
+                for image in range(slots):
+                    seen = seen + jnp.where(owner_ref[image] == slot, images_ref[block, image], 0)
+                list_ref[count] = block
+                return count + jnp.where(seen > 0, 1, 0)
+
+            count = jnp.int32(0)
+            for block in range(block_count):
+                count = collect(block, count)
+
+            def per_pair(pair, carry, piece=piece, count=count):
                 image = images[piece]
-                queries = stacked_heads(q_ref[at_block(block), :])
-                state = (state_refs[0][here, 0:1], state_refs[1][here, :], state_refs[2][here, :])
-                for start, stop in chunk_starts(image.shape[1]):
-                    keys = jnp.concatenate(
-                        [image[0, c : c + LANES, :] for c in range(start, stop, LANES)], axis=1
-                    )
+                blocks = [list_ref[2 * pair], list_ref[jnp.minimum(2 * pair + 1, count - 1)]]
+                queries = jnp.concatenate([stacked_heads(q_ref[at_block(block), :]) for block in blocks], axis=0)
+                state = [
+                    jnp.concatenate([ref[at_block(block, rows), :] for block in blocks], axis=0) for ref in state_refs
+                ]
+
+                def scores_of(chunk):
+                    start, stop = chunk
+                    keys = jnp.concatenate([image[0, c : c + LANES, :] for c in range(start, stop, LANES)], axis=1)
                     scores = jnp.dot(queries, keys, preferred_element_type=jnp.float32)
                     if stop > key_count:
                         key_id = start + lax.broadcasted_iota(jnp.int32, scores.shape, 1)
                         scores = jnp.where(key_id < key_count, scores, LOWEST)
-                    state = fold(state, scores, image[1, start:stop, :])
+                    return scores
+
+                def values_of(chunk):
+                    return image[1, chunk[0] : chunk[1], :]
+
+                state = fold_chunks(state, chunks_of(image.shape[1]), scores_of, values_of, exact)
                 for ref, value in zip(state_refs, state):
-                    ref[here, :] = jnp.broadcast_to(value, (rows, LANES))
-
-        if last:
-            total = jnp.sum(state_refs[1][...], axis=1, keepdims=True)
-            mixed = state_refs[2][...] / total
-            lse = state_refs[0][...] * LOG2_SCALE + jnp.log2(total)
+                    for index, block in enumerate(blocks):
+                        ref[at_block(block, rows), :] = value[index * rows : (index + 1) * rows]
+                return carry
+
+            lax.fori_loop(0, (count + 1) // 2, per_pair, 0)
+
+    attempt(False)
+    fine = jnp.min((jnp.max(state_refs[1][...], axis=0, keepdims=True) <= MOST_SUM).astype(jnp.int32))
+
+    @pl.when(fine == 0)
+    def _():
+        attempt(True)
+
+    if last:
+        lse_ref[...] = jnp.zeros_like(lse_ref)
+        for block in range(block_count):
+            at = slice(block * rows, (block + 1) * rows)
+            total = jnp.sum(state_refs[1][at, :], axis=1, keepdims=True)
+            mixed = state_refs[2][at, :] / total
+            lse = state_refs[0][at, :] * LOG2_SCALE + jnp.log2(total)
             for head in range(heads):
                 own = slice(head * MASK_BLOCK_TOKENS, (head + 1) * MASK_BLOCK_TOKENS)
-                out_ref[at_block(block), head * HEAD_SIZE : (head + 1) * HEAD_SIZE] = mixed[own].astype(jnp.bfloat16)
-                row = lax.broadcasted_iota(jnp.int32, (lse_ref.shape[0], MASK_BLOCK_TOKENS), 0)
-                lse_ref[:, own] = jnp.where(row == block, lse[own].T[0:1, :], lse_ref[:, own])
-        return carry
-
-    lax.fori_loop(0, block_count, per_block, 0)
-    if last:
+                here = slice(block * MASK_BLOCK_TOKENS, (block + 1) * MASK_BLOCK_TOKENS)
+                out_ref[here, head * HEAD_SIZE : (head + 1) * HEAD_SIZE] = mixed[own].astype(jnp.bfloat16)
+                lse_ref[block : block + 1, own] = lse[own].T[0:1, :]
         lse = lse_ref[...]
         first = lse.astype(jnp.bfloat16).astype(jnp.float32)
         second = (lse - first).astype(jnp.bfloat16).astype(jnp.float32)
@@ -169,13 +210,14 @@
     tokens, columns = queries.shape
     block_count = tokens // MASK_BLOCK_TOKENS
     rows = columns // HEAD_SIZE * MASK_BLOCK_TOKENS
+    state = (block_count * rows, LANES)
+    scratch = [pltpu.SMEM((block_count + 1,), jnp.int32)]
     if last:
         out_shape = jax.ShapeDtypeStruct((tokens + lse_rows(block_count), columns), jnp.bfloat16)
-        scratch = [pltpu.VMEM((-(-block_count // 8) * 8, rows), jnp.float32)]
-        scratch += [pltpu.VMEM((rows, LANES), jnp.float32)] * 3
+        scratch = [pltpu.VMEM((-(-block_count // 8) * 8, rows), jnp.float32)] + scratch
+        scratch += [pltpu.VMEM(state, jnp.float32)] * 3
     else:
-        out_shape = (jax.ShapeDtypeStruct((block_count * rows, LANES), jnp.float32),) * 3
-        scratch = []
+        out_shape = (jax.ShapeDtypeStruct(state, jnp.float32),) * 3
     flops = 4 * block_count * rows * key_count * HEAD_SIZE * len(images)
     return pl.pallas_call(
         functools.partial(cross_kernel, key_count, len(images), offset, last),
@@ -236,32 +278,41 @@
 
 def self_kernel(pieces, position_ref, q_ref, *refs):
     texts = refs[:pieces]
-    out_ref, high_ref, total_ref, mixed_ref = refs[pieces:]
+    out_ref, *state_refs = refs[pieces:]
     tokens, columns = q_ref.shape
     heads = columns // HEAD_SIZE
     rows = heads * MASK_BLOCK_TOKENS
-    state_refs = (high_ref, total_ref, mixed_ref)
     for block in range(tokens // MASK_BLOCK_TOKENS):
         start = block * MASK_BLOCK_TOKENS
         stop = start + MASK_BLOCK_TOKENS
         queries = stacked_heads(q_ref[start:stop, :])
-        scores = nt_dot(queries, texts[0][0:stop, 0:HEAD_SIZE])
-        key_id = lax.broadcasted_iota(jnp.int32, scores.shape, 1)
-        query_id = start + lax.broadcasted_iota(jnp.int32, scores.shape, 0) % MASK_BLOCK_TOKENS
-        scores = jnp.where(key_id <= query_id, scores, LOWEST)
-        state = fold(empty_state(rows), scores, texts[0][0:stop, HEAD_SIZE:])
+
+        def own_scores(chunk):
+            scores = nt_dot(queries, texts[0][0:stop, 0:HEAD_SIZE])
+            key_id = lax.broadcasted_iota(jnp.int32, scores.shape, 1)
+            query_id = start + lax.broadcasted_iota(jnp.int32, scores.shape, 0) % MASK_BLOCK_TOKENS
+            return jnp.where(key_id <= query_id, scores, LOWEST)
+
+        state = fold_chunks(
+            empty_state(rows), [(0, stop)], own_scores, lambda chunk: texts[0][0:stop, HEAD_SIZE:], True
+        )
         for ref, value in zip(state_refs, state):
-            ref[...] = jnp.broadcast_to(value, (rows, LANES))
+            ref[...] = value
         for piece in range(1, pieces):
 
             @pl.when(position_ref[0] >= piece)
             def _(piece=piece):
-                scores = nt_dot(queries, texts[piece][:, 0:HEAD_SIZE])
-                state = fold((high_ref[:, 0:1], total_ref[...], mixed_ref[...]), scores, texts[piece][:, HEAD_SIZE:])
+                state = fold_chunks(
+                    [ref[...] for ref in state_refs],
+                    [(0, tokens)],
+                    lambda chunk: nt_dot(queries, texts[piece][:, 0:HEAD_SIZE]),
+                    lambda chunk: texts[piece][:, HEAD_SIZE:],
+                    True,
+                )
                 for ref, value in zip(state_refs, state):
-                    ref[...] = jnp.broadcast_to(value, (rows, LANES))
-
-        mixed = mixed_ref[...] / jnp.sum(total_ref[...], axis=1, keepdims=True)
+                    ref[...] = value
+
+        mixed = state_refs[2][...] / jnp.sum(state_refs[1][...], axis=1, keepdims=True)
         for head in range(heads):
             out_ref[start:stop, head * HEAD_SIZE : (head + 1) * HEAD_SIZE] = mixed[
                 head * MASK_BLOCK_TOKENS : (head + 1) * MASK_BLOCK_TOKENS
@@ -305,23 +356,28 @@
     queries = {step: shifted(cross_queries, "enc", ring - step) for step in order}
     queries[0] = cross_queries
 
+    text = text_kv.reshape(rows, 2 * HEAD_SIZE)
+    texts = [text]
+    for step in range(1, cycle):
+        texts.append(lax.ppermute(texts[-1], "blk", [(source, source + 1) for source in range(cycle - 1)]))
+
     alone = cycle == 1
-    states = {}
-    for step in [0] + order:
-        states[step] = () if alone else cross_part(tables, queries[step], images[:1], key_count, 0, False)
+    states = {0: ()}
+    if not alone:
+        states[0] = cross_part(tables, queries[0], images[:1], key_count, 0, False)
+    earlier = states[0]
+    for step in order:
+        if alone:
+            states[step] = ()
+        else:
+            queries[step], _ = lax.optimization_barrier((queries[step], earlier))
+            earlier = states[step] = cross_part(tables, queries[step], images[:1], key_count, 0, False)
 
     def finished(step):
         offset = 0 if alone else 1
         return cross_part(tables, queries[step], images[offset:], key_count, offset, True, states[step])
 
     received = [shifted(finished(step), "enc", step) for step in order]
-
-    text = text_kv.reshape(rows, 2 * HEAD_SIZE)
-    after, _ = lax.optimization_barrier((text, images[-1]))
-    texts = [text]
-    for step in range(1, cycle):
-        after = lax.ppermute(after, "blk", [(source, source + 1) for source in range(cycle - 1)])
-        texts.append(after)
 
     own = finished(0)
     self_out = self_attention(position, self_queries, texts)

time: 75.5 us -> 64.7 us (0.86)
  the two profiles are of different devices: /device:TPU:6 before, /device:TPU:23 now
where the time goes in v2:
time: 64.7 us; the launch traced here: 65 us
  Pallas kernels  36.9 us (57%)
  waiting for transfers between devices  15.7 us (24%)
  starting transfers between devices  8.43 us (13%)
  local copies, waits for them, and re-layouts  3.14 us (5%)
  between operations  0.77 us (1%)
    pallas_call x8, Pallas kernels, cross_part(): pl.pallas_call(functools.partial(cross_kernel, key_count, len(images), of...  30.5 us
    ppermute x7, waiting for transfers between devices, shifted(): lax.ppermute(value, axis, [(source, (source + steps) % count) for source...  15.7 us
    ppermute x7, starting transfers between devices, shifted(): lax.ppermute(value, axis, [(source, (source + steps) % count) for source...  7.14 us
    pallas_call x1, Pallas kernels, self_attention(): pl.pallas_call(functools.partial(self_kernel, pieces), out_shape=jax.Shap...  4.72 us
    unnamed x13, local copies, waits for them, and re-layouts  3.14 us
    pallas_call x1, Pallas kernels, combined(): pl.pallas_call(functools.partial(combine_kernel, len(parts)), out_shape=j...  1.52 us
  transfers between devices with their start and end apart: 8, of which 4 were waited for; matrix products, arithmetic and copies ran while one was open for 0% of the time, Pallas kernels for 54%

profile of v2, /device:TPU:23, one launch (start us, length us, event | category | flops | bytes accessed | tf_op | source)
XLA Modules:
  0.0 65.0 jit_solution(6541381521812007638)
XLA Ops:
  0.6 1.3 %copy.20 = bf16[1,2,1601,128]{3,2,1,0:T(8,128)(2,1)S(1)} copy(bf16[1,2,1601,128]{3,1,2,0:T(2,128)(2,1)} %param.9) | data formatting | bytes 1639424 | tf_op args[3]
  1.9 0.0 copy-start.1
  1.9 0.0 copy-start.3
  1.9 0.2 prepare.1.refs_0_
  2.1 0.3 collective-permute-start.1
  2.4 0.4 copy-done.1
  2.8 0.1 collective-permute-start.2
  2.9 2.4 %collective-permute-start.4 = (bf16[512,256]{1,0:T(8,128)(2,1)S(1)}, bf16[512,256]{1,0:T(8,128)(2,1)S(1)}, u32[]{:S(2)}, u32[]{:S(2)}) collective-permute-start(bf16[512,256]{1,0:T(8,128)(2,1)S(1)} %copy-done.1), channel_id=1, source_target_pairs={{0,3},{1,0},{2,1},{3,2},{4,7},{5,4},{6,5},{7,6},{8,11},{9,8},{10,9... | collective-permute-start | bytes 786440 | tf_op jit(solution)/shard_map/ppermute | solution.py:340
  5.3 0.0 collective-permute-start.6
  5.3 0.0 copy-done.3
  5.4 1.3 %collective-permute-start = (bf16[512,256]{1,0:T(8,128)(2,1)S(1)}, bf16[512,256]{1,0:T(8,128)(2,1)S(1)}, u32[]{:S(2)}, u32[]{:S(2)}) collective-permute-start(bf16[512,256]{1,0:T(8,128)(2,1)S(1)} %bitcast.9), channel_id=1, source_target_pairs={{0,16},{1,17},{2,18},{3,19},{4,20},{5,21},{6,22},{7,23},{8,24},{9,... | collective-permute-start | bytes 786440 | tf_op jit(solution)/shard_map/ppermute | solution.py:362
  6.7 0.0 copy-start.4
  6.7 0.7 %copy-done.4 = s32[4,2]{0,1:T(2,128)S(1)} copy-done((s32[4,2]{0,1:T(2,128)S(1)}, s32[4,2]{0,1:T(2,128)}, u32[]{:S(2)}) %copy-start.4) | copy-done | bytes 56
  7.4 0.1 copy.10.images_ref
  7.4 0.0 copy-start.2
  7.4 0.7 %copy-done.2 = s32[2]{0:T(128)S(1)} copy-done((s32[2]{0:T(128)S(1)}, s32[2]{0:T(128)}, u32[]{:S(2)}) %copy-start.2) | copy-done | bytes 32
  8.1 3.7 %cross_first.4 = (f32[1024,128]{1,0:T(8,128)S(1)}, f32[1024,128]{1,0:T(8,128)S(1)}, f32[1024,128]{1,0:T(8,128)S(1)}) custom-call(s32[1]{0:T(128)} %bitcast.position_ref, s32[4,2]{1,0:T(4,128)S(1)} %copy.10.images_ref, s32[2]{0:T(128)S(1)} %copy-done.2, bf16[512,256]{1,0:T(8,128)(2,1)S(1)} %copy-done.1, bf16[2,1664,128]{2,1,0:T(8,128)(2,1)S(1)} %prepare.1.refs_0_), custom_call_target="tpu_custom_call" | custom-call | flops 1678770176 | bytes 4194304 | tf_op jit(solution)/shard_map/cross_first/pallas_call | solution.py:222
  11.8 1.8 %collective-permute-done.2.q_ref = bf16[512,256]{1,0:T(8,128)(2,1)S(1)} collective-permute-done((bf16[512,256]{1,0:T(8,128)(2,1)S(1)}, bf16[512,256]{1,0:T(8,128)(2,1)S(1)}, u32[]{:S(2)}, u32[]{:S(2)}) %collective-permute-start.2) | collective-permute-done | bytes 262176 | tf_op jit(solution)/shard_map/ppermute | solution.py:340
  13.6 3.7 %cross_first.5 = (f32[1024,128]{1,0:T(8,128)S(1)}, f32[1024,128]{1,0:T(8,128)S(1)}, f32[1024,128]{1,0:T(8,128)S(1)}) custom-call(s32[1]{0:T(128)} %bitcast.position_ref, s32[4,2]{1,0:T(4,128)S(1)} %copy.10.images_ref, s32[2]{0:T(128)S(1)} %copy-done.2, bf16[512,256]{1,0:T(8,128)(2,1)S(1)} %collective-permute-done.2.q_ref, ...), custom_call_target="tpu_custom_call" | custom-call | flops 1678770176 | bytes 4194304 | tf_op jit(solution)/shard_map/cross_first/pallas_call | solution.py:222
  17.2 7.5 %collective-permute-done.4.q_ref = bf16[512,256]{1,0:T(8,128)(2,1)S(1)} collective-permute-done((bf16[512,256]{1,0:T(8,128)(2,1)S(1)}, bf16[512,256]{1,0:T(8,128)(2,1)S(1)}, u32[]{:S(2)}, u32[]{:S(2)}) %collective-permute-start.4) | collective-permute-done | bytes 262176 | tf_op jit(solution)/shard_map/ppermute | solution.py:340
  24.8 3.7 %cross_first.6 = (f32[1024,128]{1,0:T(8,128)S(1)}, f32[1024,128]{1,0:T(8,128)S(1)}, f32[1024,128]{1,0:T(8,128)S(1)}) custom-call(s32[1]{0:T(128)} %bitcast.position_ref, s32[4,2]{1,0:T(4,128)S(1)} %copy.10.images_ref, s32[2]{0:T(128)S(1)} %copy-done.2, bf16[512,256]{1,0:T(8,128)(2,1)S(1)} %collective-permute-done.4.q_ref, ...), custom_call_target="tpu_custom_call" | custom-call | flops 1678770176 | bytes 4194304 | tf_op jit(solution)/shard_map/cross_first/pallas_call | solution.py:222
  28.5 0.4 collective-permute-done.6.q_ref
  28.9 3.8 %cross_first.7 = (f32[1024,128]{1,0:T(8,128)S(1)}, f32[1024,128]{1,0:T(8,128)S(1)}, f32[1024,128]{1,0:T(8,128)S(1)}) custom-call(s32[1]{0:T(128)} %bitcast.position_ref, s32[4,2]{1,0:T(4,128)S(1)} %copy.10.images_ref, s32[2]{0:T(128)S(1)} %copy-done.2, bf16[512,256]{1,0:T(8,128)(2,1)S(1)} %collective-permute-done.6.q_ref, ...), custom_call_target="tpu_custom_call" | custom-call | flops 1678770176 | bytes 4194304 | tf_op jit(solution)/shard_map/cross_first/pallas_call | solution.py:222
  32.7 0.0 collective-permute-done.1.refs_0_
  32.7 3.9 %cross_last.5 = bf16[528,256]{1,0:T(8,128)(2,1)S(1)} custom-call(s32[1]{0:T(128)} %bitcast.position_ref, s32[4,2]{1,0:T(4,128)S(1)} %copy.10.images_ref, s32[2]{0:T(128)S(1)} %copy-done.2, bf16[512,256]{1,0:T(8,128)(2,1)S(1)} %collective-permute-done.2.q_ref, bf16[2,1664,128]{2,1,0:T(8,128)(2,1)S(1)} %collective-permute-done.1.refs_0_, ...), custom_call_target="tpu_custom_call" | custom-call | flops 1678770176 | bytes 4194304 | tf_op jit(solution)/shard_map/cross_last/pallas_call | solution.py:222
  36.6 0.1 collective-permute-start.3
  36.7 3.9 %cross_last.6 = bf16[528,256]{1,0:T(8,128)(2,1)S(1)} custom-call(s32[1]{0:T(128)} %bitcast.position_ref, s32[4,2]{1,0:T(4,128)S(1)} %copy.10.images_ref, s32[2]{0:T(128)S(1)} %copy-done.2, bf16[512,256]{1,0:T(8,128)(2,1)S(1)} %collective-permute-done.4.q_ref, bf16[2,1664,128]{2,1,0:T(8,128)(2,1)S(1)} %collective-permute-done.1.refs_0_, ...), custom_call_target="tpu_custom_call" | custom-call | flops 1678770176 | bytes 4194304 | tf_op jit(solution)/shard_map/cross_last/pallas_call | solution.py:222
  40.6 3.0 %collective-permute-start.5 = (bf16[528,256]{1,0:T(8,128)(2,1)S(1)}, bf16[528,256]{1,0:T(8,128)(2,1)S(1)}, u32[]{:S(2)}, u32[]{:S(2)}) collective-permute-start(bf16[528,256]{1,0:T(8,128)(2,1)S(1)} %cross_last.6), channel_id=1, source_target_pairs={{0,1},{1,2},{2,3},{3,0},{4,5},{5,6},{6,7},{7,4},{8,9},{9,10},{10,1... | collective-permute-start | bytes 811016 | tf_op jit(solution)/shard_map/ppermute | solution.py:340
  43.7 0.0 copy-start
  43.7 3.9 %cross_last.7 = bf16[528,256]{1,0:T(8,128)(2,1)S(1)} custom-call(s32[1]{0:T(128)} %bitcast.position_ref, s32[4,2]{1,0:T(4,128)S(1)} %copy.10.images_ref, s32[2]{0:T(128)S(1)} %copy-done.2, bf16[512,256]{1,0:T(8,128)(2,1)S(1)} %collective-permute-done.6.q_ref, bf16[2,1664,128]{2,1,0:T(8,128)(2,1)S(1)} %collective-permute-done.1.refs_0_, ...), custom_call_target="tpu_custom_call" | custom-call | flops 1678770176 | bytes 4194304 | tf_op jit(solution)/shard_map/cross_last/pallas_call | solution.py:222
  47.6 1.2 %collective-permute-start.7 = (bf16[528,256]{1,0:T(8,128)(2,1)S(1)}, bf16[528,256]{1,0:T(8,128)(2,1)S(1)}, u32[]{:S(2)}, u32[]{:S(2)}) collective-permute-start(bf16[528,256]{1,0:T(8,128)(2,1)S(1)} %cross_last.7), channel_id=1, source_target_pairs={{0,3},{1,0},{2,1},{3,2},{4,7},{5,4},{6,5},{7,6},{8,11},{9,8},{10,9... | collective-permute-start | bytes 811016 | tf_op jit(solution)/shard_map/ppermute | solution.py:340
  48.8 0.0 collective-permute-done.refs_1_
  48.8 0.0 copy-done
  48.8 4.7 %self_attention.1 = bf16[512,256]{1,0:T(8,128)(2,1)} custom-call(s32[1]{0:T(128)} %bitcast.position_ref, bf16[512,256]{1,0:T(8,128)(2,1)S(1)} %copy-done, bf16[512,256]{1,0:T(8,128)(2,1)S(1)} %bitcast.10, bf16[512,256]{1,0:T(8,128)(2,1)S(1)} %collective-permute-done.refs_1_), custom_call_target="tpu_custom_call" | custom-call | flops 536870912 | bytes 1048576 | tf_op jit(solution)/shard_map/self_attention/pallas_call | solution.py:326
  53.5 3.9 %cross_last.4.refs_0_ = bf16[528,256]{1,0:T(8,128)(2,1)S(1)} custom-call(s32[1]{0:T(128)} %bitcast.position_ref, s32[4,2]{1,0:T(4,128)S(1)} %copy.10.images_ref, s32[2]{0:T(128)S(1)} %copy-done.2, bf16[512,256]{1,0:T(8,128)(2,1)S(1)} %copy-done.1, bf16[2,1664,128]{2,1,0:T(8,128)(2,1)S(1)} %collective-permute-done.1.refs_0_, ...), custom_call_target="tpu_custom_call" | custom-call | flops 1678770176 | bytes 4194304 | tf_op jit(solution)/shard_map/cross_last/pallas_call | solution.py:222
  57.5 0.0 collective-permute-done.3.refs_1_
  57.5 6.0 %collective-permute-done.5.refs_2_ = bf16[528,256]{1,0:T(8,128)(2,1)S(1)} collective-permute-done((bf16[528,256]{1,0:T(8,128)(2,1)S(1)}, bf16[528,256]{1,0:T(8,128)(2,1)S(1)}, u32[]{:S(2)}, u32[]{:S(2)}) %collective-permute-start.5) | collective-permute-done | bytes 270368 | tf_op jit(solution)/shard_map/ppermute | solution.py:340
  63.4 0.0 collective-permute-done.7.refs_3_
  63.4 1.5 %combine.1 = bf16[512,256]{1,0:T(8,128)(2,1)} custom-call(bf16[528,256]{1,0:T(8,128)(2,1)S(1)} %cross_last.4.refs_0_, bf16[528,256]{1,0:T(8,128)(2,1)S(1)} %collective-permute-done.3.refs_1_, bf16[528,256]{1,0:T(8,128)(2,1)S(1)} %collective-permute-done.5.refs_2_, bf16[528,256]{1,0:T(8,128)(2,1)S(1)} %collective-permute-done.7.refs_3_), custom_call_target="tpu_custom_call" | custom-call | bytes 2097152 | tf_op jit(solution)/shard_map/combine/pallas_call | solution.py:268
  (1 shorter events, 0.0 us)
Async XLA Ops:
  1.9 1.0 %copy-start.1 = (bf16[512,256]{1,0:T(8,128)(2,1)S(1)}, bf16[512,256]{1,0:T(8,128)(2,1)}, u32[]{:S(2)}) copy-start(bf16[512,256]{1,0:T(8,128)(2,1)} %q_ref.5) | copy-start | bytes 786436
  1.9 3.4 %copy-start.3 = (bf16[512,2,128]{2,1,0:T(2,128)(2,1)S(1)}, bf16[512,2,128]{2,1,0:T(2,128)(2,1)}, u32[]{:S(2)}) copy-start(bf16[512,2,128]{2,1,0:T(2,128)(2,1)} %param.7) | copy-start | bytes 786436
  2.1 30.6 %collective-permute-start.1 = (bf16[2,1664,128]{2,1,0:T(8,128)(2,1)S(1)}, bf16[2,1664,128]{2,1,0:T(8,128)(2,1)S(1)}, u32[]{:S(2)}, u32[]{:S(2)}) collective-permute-start(bf16[2,1664,128]{2,1,0:T(8,128)(2,1)S(1)} %prepare.1.refs_0_), channel_id=1, source_target_pairs={{0,16},{16,0},{1,17},{17,1},{2,18},{18,2},{3,19},{19,3},{4,20},{20... | collective-permute-start | bytes 2555912 | tf_op jit(solution)/shard_map/ppermute | solution.py:340
  2.8 10.7 %collective-permute-start.2 = (bf16[512,256]{1,0:T(8,128)(2,1)S(1)}, bf16[512,256]{1,0:T(8,128)(2,1)S(1)}, u32[]{:S(2)}, u32[]{:S(2)}) collective-permute-start(bf16[512,256]{1,0:T(8,128)(2,1)S(1)} %copy-done.1), channel_id=1, source_target_pairs={{0,2},{1,3},{2,0},{3,1},{4,6},{5,7},{6,4},{7,5},{8,10},{9,11},{10,... | collective-permute-start | bytes 786440 | tf_op jit(solution)/shard_map/ppermute | solution.py:340
  2.9 21.9 %collective-permute-start.4 = (bf16[512,256]{1,0:T(8,128)(2,1)S(1)}, bf16[512,256]{1,0:T(8,128)(2,1)S(1)}, u32[]{:S(2)}, u32[]{:S(2)}) collective-permute-start(bf16[512,256]{1,0:T(8,128)(2,1)S(1)} %copy-done.1), channel_id=1, source_target_pairs={{0,3},{1,0},{2,1},{3,2},{4,7},{5,4},{6,5},{7,6},{8,11},{9,8},{10,9... | collective-permute-start | bytes 786440 | tf_op jit(solution)/shard_map/ppermute | solution.py:340
  5.3 23.5 %collective-permute-start.6 = (bf16[512,256]{1,0:T(8,128)(2,1)S(1)}, bf16[512,256]{1,0:T(8,128)(2,1)S(1)}, u32[]{:S(2)}, u32[]{:S(2)}) collective-permute-start(bf16[512,256]{1,0:T(8,128)(2,1)S(1)} %copy-done.1), channel_id=1, source_target_pairs={{0,1},{1,2},{2,3},{3,0},{4,5},{5,6},{6,7},{7,4},{8,9},{9,10},{10,1... | collective-permute-start | bytes 786440 | tf_op jit(solution)/shard_map/ppermute | solution.py:340
  5.4 43.5 %collective-permute-start = (bf16[512,256]{1,0:T(8,128)(2,1)S(1)}, bf16[512,256]{1,0:T(8,128)(2,1)S(1)}, u32[]{:S(2)}, u32[]{:S(2)}) collective-permute-start(bf16[512,256]{1,0:T(8,128)(2,1)S(1)} %bitcast.9), channel_id=1, source_target_pairs={{0,16},{1,17},{2,18},{3,19},{4,20},{5,21},{6,22},{7,23},{8,24},{9,... | collective-permute-start | bytes 786440 | tf_op jit(solution)/shard_map/ppermute | solution.py:362
  6.7 0.7 %copy-start.4 = (s32[4,2]{0,1:T(2,128)S(1)}, s32[4,2]{0,1:T(2,128)}, u32[]{:S(2)}) copy-start(s32[4,2]{0,1:T(2,128)} %param.10) | copy-start | bytes 100
  7.4 0.7 %copy-start.2 = (s32[2]{0:T(128)S(1)}, s32[2]{0:T(128)}, u32[]{:S(2)}) copy-start(s32[2]{0:T(128)} %owner_ref.15) | copy-start | bytes 28
  36.6 20.8 %collective-permute-start.3 = (bf16[528,256]{1,0:T(8,128)(2,1)S(1)}, bf16[528,256]{1,0:T(8,128)(2,1)S(1)}, u32[]{:S(2)}, u32[]{:S(2)}) collective-permute-start(bf16[528,256]{1,0:T(8,128)(2,1)S(1)} %cross_last.5), channel_id=1, source_target_pairs={{0,2},{1,3},{2,0},{3,1},{4,6},{5,7},{6,4},{7,5},{8,10},{9,11},{10,... | collective-permute-start | bytes 811016 | tf_op jit(solution)/shard_map/ppermute | solution.py:340
  40.6 22.8 %collective-permute-start.5 = (bf16[528,256]{1,0:T(8,128)(2,1)S(1)}, bf16[528,256]{1,0:T(8,128)(2,1)S(1)}, u32[]{:S(2)}, u32[]{:S(2)}) collective-permute-start(bf16[528,256]{1,0:T(8,128)(2,1)S(1)} %cross_last.6), channel_id=1, source_target_pairs={{0,1},{1,2},{2,3},{3,0},{4,5},{5,6},{6,7},{7,4},{8,9},{9,10},{10,1... | collective-permute-start | bytes 811016 | tf_op jit(solution)/shard_map/ppermute | solution.py:340
  43.7 5.1 %copy-start = (bf16[512,256]{1,0:T(8,128)(2,1)S(1)}, bf16[512,256]{1,0:T(8,128)(2,1)}, u32[]{:S(2)}) copy-start(bf16[512,256]{1,0:T(8,128)(2,1)} %q_ref.3) | copy-start | bytes 786436
  47.6 15.8 %collective-permute-start.7 = (bf16[528,256]{1,0:T(8,128)(2,1)S(1)}, bf16[528,256]{1,0:T(8,128)(2,1)S(1)}, u32[]{:S(2)}, u32[]{:S(2)}) collective-permute-start(bf16[528,256]{1,0:T(8,128)(2,1)S(1)} %cross_last.7), channel_id=1, source_target_pairs={{0,3},{1,0},{2,1},{3,2},{4,7},{5,4},{6,5},{7,6},{8,11},{9,8},{10,9... | collective-permute-start | bytes 811016 | tf_op jit(solution)/shard_map/ppermute | solution.py:340
